TPU v7x, 32 devices: a whole 2x2x4 slice. The times are simulated.
32 devices in a mesh: ctx: 8 (over z, x), head: 4 (over y, core).
Axes of the slice: x: 2, y: 2, z: 4, core: 2. Of those that a mesh axis runs over, the one named last changes fastest.
Arguments:
- queries: bfloat16 [2048, 4096], P('ctx', 'head'), may hold values from -6 to 6
- keys: bfloat16 [2048, 2, 4096], P('ctx', None, 'head'), may hold values from -6 to 6
- values: bfloat16 [2048, 2, 4096], P('ctx', None, 'head'), may hold values from -6 to 6
- betas: float32 [2, 32, 2048], P(None, 'head', 'ctx'), may hold values from 0.02 to 1.9
- log_decay: float32 [32, 2048], P('head', 'ctx'), may hold values from -1 to 0
- segment: int32 [2048], P('ctx'), may hold values from 0 to 15, never falling along the last dimension, each value on 1 to 1024 neighbouring positions
- gain: float32 [4096], P('head'), may hold values from 0.1 to 1.9
- out_weight: bfloat16 [4096, 4096], P('head'), may hold values from -0.125 to 0.125
Outputs:
- mixed: bfloat16 [2048, 4096], P('ctx', 'head')
Inputs may be any that keep to these rules, and one draw needn't show every extreme that they name: `segment`: document numbers never fall along the context; every document has 1 to 1024 tokens and one has exactly 1024.
All inputs are finite; a program needn't handle non-finite values.
Results may differ from a plain program's by a relative error of at most 0.0049.
Values sent between devices are 32-bit elements; how exact they have to be, the bound alone decides.
A program may use at most 192 MiB of HBM per device.

v0:
```python
import jax
import jax.numpy as jnp
from jax import lax
from jax.sharding import PartitionSpec as P

DK = 128
DV = 128
GROUP = 64


HIGHEST = lax.Precision.HIGHEST


def shifted(value, axis, steps):
    count = lax.axis_size(axis)
    initial, last = (max(0, -steps), min(count, count - steps))
    return lax.ppermute(value, axis, [(source, source + steps) for source in range(initial, last)])


def unit_rows(matrix):
    return matrix / jnp.sqrt(jnp.sum(matrix * matrix, axis=-1, keepdims=True) + 1e-06)


def shards(queries, keys, values, betas, log_decay, segment, gain, out_weight):
    tok_local = queries.shape[0]
    heads_local = betas.shape[1]
    blocks = tok_local // GROUP
    rows = 2 * GROUP
    query_unit = unit_rows(queries.astype(jnp.float32).reshape(blocks, GROUP, heads_local, DK))
    query_unit = jnp.transpose(query_unit, (2, 0, 1, 3))
    key_unit = unit_rows(keys.astype(jnp.float32).reshape(blocks, rows, heads_local, DK))
    key_unit = jnp.transpose(key_unit, (2, 0, 1, 3))
    value_rows = jnp.transpose(
        values.astype(jnp.float32).reshape(blocks, rows, heads_local, DV), (2, 0, 1, 3)
    )
    strengths = jnp.transpose(betas.reshape(2, heads_local, blocks, GROUP), (1, 2, 3, 0)).reshape(
        heads_local, blocks, rows
    )
    token_log = log_decay.reshape(heads_local, blocks, GROUP)
    step_log = jnp.stack([token_log, jnp.zeros_like(token_log)], axis=-1).reshape(
        heads_local, blocks, rows
    )
    cumulative = jnp.cumsum(step_log, axis=-1)
    penultimate_state = shifted(segment[tok_local - 1 :], "ctx", 1)
    seg_blocks = segment.reshape(blocks, GROUP)
    row_seg = jnp.repeat(seg_blocks, 2, axis=1)
    group_prior = jnp.concatenate([penultimate_state, seg_blocks[:-1, GROUP - 1]])
    position = jnp.arange(rows)
    causal = position[:, None] >= position[None, :]
    strictly = position[:, None] > position[None, :]
    same_doc = row_seg[:, :, None] == row_seg[:, None, :]
    linked = same_doc & causal[None, :, :]
    earlier_link = same_doc & strictly[None, :, :]
    spread_log = cumulative[..., :, None] - cumulative[..., None, :]
    within = jnp.where(linked[None], jnp.exp(jnp.where(linked[None], spread_log, 0.0)), 0.0)
    entry = jnp.where((row_seg == group_prior[:, None])[None], jnp.exp(cumulative), 0.0)
    intersections = jnp.einsum("hnrd,hnsd->hnrs", key_unit, key_unit, precision=HIGHEST)
    lower_part = jnp.where(
        earlier_link[None], strengths[..., :, None] * within * intersections, 0.0
    )
    system = lower_part + jnp.eye(rows, dtype=jnp.float32)
    right_side = jnp.concatenate(
        [strengths[..., None] * value_rows, (strengths * entry)[..., None] * key_unit], axis=-1
    )
    solved = lax.linalg.triangular_solve(
        system, right_side, left_side=True, lower=True, unit_diagonal=True
    )
    pseudo = solved[..., :DV]
    key_mix = solved[..., DV:]
    within_query = within[:, :, 1::2, :]
    entry_query = entry[:, :, 1::2]
    scores = jnp.einsum("hnid,hnsd->hnis", query_unit, key_unit, precision=HIGHEST) * within_query
    local_out = jnp.einsum("hnis,hnsv->hniv", scores, pseudo, precision=HIGHEST)
    reach = entry_query[..., None] * query_unit - jnp.einsum(
        "hnis,hnsd->hnid", scores, key_mix, precision=HIGHEST
    )
    tail = within[:, :, rows - 1, :]
    tail_entry = entry[:, :, rows - 1]
    transition = tail_entry[..., None, None] * jnp.eye(DK, dtype=jnp.float32) - jnp.einsum(
        "hnsa,hnsb->hnab", key_mix * tail[..., None], key_unit, precision=HIGHEST
    )
    addition = jnp.einsum("hnsv,hnsb->hnvb", pseudo * tail[..., None], key_unit, precision=HIGHEST)

    def compose(running, block_pair):
        block_map, block_add = block_pair
        next_map = jnp.einsum("hab,hbc->hac", running[0], block_map, precision=HIGHEST)
        next_add = jnp.einsum("hvb,hbc->hvc", running[1], block_map, precision=HIGHEST) + block_add
        return ((next_map, next_add), running)

    identity_map = jnp.broadcast_to(jnp.eye(DK, dtype=jnp.float32), (heads_local, DK, DK))
    empty_state = jnp.zeros((heads_local, DV, DK), jnp.float32)
    device_pair, prefixes = lax.scan(
        compose,
        (identity_map, empty_state),
        (jnp.moveaxis(transition, 1, 0), jnp.moveaxis(addition, 1, 0)),
    )
    prefix_map = jnp.moveaxis(prefixes[0], 0, 1)
    prefix_add = jnp.moveaxis(prefixes[1], 0, 1)
    mapped = jnp.einsum("hnik,hnak->hnia", reach, prefix_map, precision=HIGHEST)
    local_out = local_out + jnp.einsum("hnik,hnvk->hniv", reach, prefix_add, precision=HIGHEST)
    turns = min(8, lax.axis_size("ctx") // 2)

    def relay(turn, state_pair):
        arrived = shifted(state_pair[1], "ctx", 1)
        leaving = (
            jnp.einsum("hva,hab->hvb", arrived, device_pair[0], precision=HIGHEST) + device_pair[1]
        )
        return (arrived, leaving)

    incoming, leaving_last = lax.fori_loop(0, turns, relay, (empty_state, device_pair[1]))
    attended = local_out + jnp.einsum("hnia,hva->hniv", mapped, incoming, precision=HIGHEST)
    attended = jnp.transpose(attended, (1, 2, 0, 3)).reshape(tok_local, heads_local, DV)
    inverse_rms = 1.0 / jnp.sqrt(jnp.mean(attended * attended, axis=-1, keepdims=True) + 1e-06)
    normed = ((attended * inverse_rms).reshape(tok_local, heads_local * DV) * gain[None, :]).astype(
        jnp.bfloat16
    )
    terms = jnp.dot(normed, out_weight, preferred_element_type=jnp.float32)
    return lax.psum_scatter(terms, "head", scatter_dimension=1, tiled=True).astype(jnp.bfloat16)


def solution(mesh):
    return jax.shard_map(
        shards,
        mesh=mesh,
        in_specs=(
            P("ctx", "head"),
            P("ctx", None, "head"),
            P("ctx", None, "head"),
            P(None, "head", "ctx"),
            P("head", "ctx"),
            P("ctx"),
            P("head"),
            P("head", None),
        ),
        out_specs=P("ctx", "head"),
        check_vma=False,
    )
```

profile of v0, /device:TPU:27, one launch (start us, length us, event | category | flops | bytes accessed | tf_op | source)
XLA Modules:
  0.0 548.0 jit_solution(11448406333828805239)
XLA Ops:
  17.9 2.8 slice.28
  23.1 1.6 reshape.149
  25.5 2.7 reshape.150
  28.4 6.6 %add_bitcast_fusion = f32[8,4,1,128,128]{4,3,2,1,0:T(8,128)} fusion(f32[128,128]{1,0:T(8,128)S(1)} %copy-done.14, f32[128,128]{1,0:T(8,128)S(1)} %get-tuple-element.219, f32[8,4,128]{2,1,0:T(4,128)S(1)} %copy-done.13, pred[4,128,128]{2,1,0:T(8,128)(4,1)S(1)} %copy-done.16, pred[128,128]{1,0:T(8,128)(4,1)S(1)} %get-tuple-element.218, ...), kind=kOutput, calls=%fused_computation.40 | convolution fusion | flops 810549248 | bytes 4521984 | tf_op jit(solution)/shard_map/hnrd,hnsd->hnrs/dot_general | solution.py:57
  35.0 315.8 %custom-call.3 = f32[8,4,1,128,128]{3,4,2,1,0:T(8,128)} custom-call(f32[8,4,1,128,128]{4,3,2,1,0:T(8,128)} %add_bitcast_fusion), custom_call_target="InvertDiagBlocksLowerTriangular" | custom-call | tf_op jit(solution)/shard_map/triangular_solve | solution.py:65
  350.8 7.0 %fusion.53 = f32[8,4,64,128]{3,2,1,0:T(8,128)} fusion(f32[8,4,64,128]{3,2,1,0:T(8,128)} %slice.28, f32[4,64,8,128]{3,2,1,0:T(8,128)} %bitcast.129, f32[4,64,8]{1,0,2:T(4,128)S(1)} %copy.200, f32[4,128,8,128]{3,2,1,0:T(8,128)S(1)} %reshape.149, f32[4,128,8]{1,0,2:T(4,128)S(1)} %copy.203), kind=kOutput, calls=%fused_computation.52 | convolution fusion | flops 403701760 | bytes 5267456 | tf_op jit(solution)/shard_map/hnid,hnsd->hnis/dot_general | solution.py:72
  359.3 3.9 bitcast_multiply_fusion
  363.2 3.8 fusion.11
  367.0 6.1 %fusion.38 = f32[4,8,128,128]{3,2,0,1:T(8,128)} fusion(f32[8,4,128,256]{3,2,1,0:T(8,128)S(1)} %fusion.11, f32[8,4,128]{2,1,0:T(4,128)S(1)} %bitcast.140, f32[4,128,8,128]{3,2,1,0:T(8,128)S(1)} %reshape.149, f32[4,128,8]{1,0,2:T(4,128)S(1)} %copy.203), kind=kOutput, calls=%fused_computation.49 | convolution fusion | flops 806354944 | bytes 6324224 | tf_op jit(solution)/shard_map/hnsv,hnsb->hnvb/dot_general | solution.py:82
  373.2 6.2 %bitcast_subtract_fusion = f32[4,8,128,128]{3,2,0,1:T(8,128)} fusion(f32[8,4,128,256]{3,2,1,0:T(8,128)S(1)} %fusion.11, f32[8,4,128]{2,1,0:T(4,128)S(1)} %bitcast.141, f32[128,128]{1,0:T(8,128)S(1)} %get-tuple-element.219, f32[4,8]{0,1:T(8,128)S(1)} %copy.221, f32[4,128,8,128]{3,2,1,0:T(8,128)S(1)} %reshape.149, f32[4,128,8]{1,0,2:T(4,128)S(1)} %copy.203), kind=kOutput, calls=%fused_computation.25 | convolution fusion | flops 807403520 | bytes 6393856 | tf_op jit(solution)/shard_map/hnsa,hnsb->hnab/dot_general | solution.py:79
  379.4 26.7 %while.30 = (s32[]{:T(128)}, f32[8,128,128]{1,2,0:T(8,128)S(1)}, f32[8,128,128]{1,2,0:T(8,128)S(1)}, f32[4,8,128,128]{2,3,1,0:T(8,128)}, f32[4,8,128,128]{2,3,1,...) while((s32[]{:T(128)}, f32[8,128,128]{1,2,0:T(8,128)S(1)}, ...), condition=%wide.region_4.5_spmd.clone, body=%wide.region_3.4_spmd.clone.sunk | while | flops 403046400 | bytes 9961600 | solution.py:92
  380.6 2.1 convolution_bitcast_fusion.3
  383.9 2.1 fusion.96
  387.2 2.1 convolution_bitcast_fusion.3
  390.5 2.1 fusion.96
  393.8 2.1 convolution_bitcast_fusion.3
  397.1 2.1 fusion.96
  400.4 2.1 convolution_bitcast_fusion.3
  403.8 2.1 fusion.96
  406.1 4.3 fusion.50
  410.4 2.1 fusion.17
  412.6 2.1 fusion.47
  414.7 3.1 fusion.15
  418.2 58.8 %while.29 = (s32[]{:T(128)}, f32[8,128,128]{2,1,0:T(8,128)}, f32[8,128,128]{2,1,0:T(8,128)S(1)}, f32[8,128,128]{2,1,0:T(8,128)S(1)}, f32[8,128,128]{2,1,0:T(8,128)S(1)}, /*index=5*/s32[]{:T(128)}) while((s32[]{:T(128)}, f32[8,128,128]{2,1,0:T(8,128)}, f32[8,128,128]{2,1,0:T(8,128)S(1)}, f32[8,128,128]{2,1,0:T(8,128)S(1)}, ...), condition=%wide.region_6.7_spmd, body=%wide.region_5.6_spmd.sunk | while | flops 201457664 | bytes 6291593 | solution.py:110
  419.5 14.0 %collective-permute-done = f32[8,128,128]{2,1,0:T(8,128)S(1)} collective-permute-done((f32[8,128,128]{2,1,0:T(8,128)S(1)}, f32[8,128,128]{2,1,0:T(8,128)S(1)}, u32[]{:S(2)}, u32[]{:S(2)}) %collective-permute-start) | collective-permute-done | bytes 524320 | tf_op jit(solution)/shard_map/while/body/eval_jaxpr/ppermute | solution.py:17
  435.6 13.0 %collective-permute-done = f32[8,128,128]{2,1,0:T(8,128)S(1)} collective-permute-done((f32[8,128,128]{2,1,0:T(8,128)S(1)}, f32[8,128,128]{2,1,0:T(8,128)S(1)}, u32[]{:S(2)}, u32[]{:S(2)}) %collective-permute-start) | collective-permute-done | bytes 524320 | tf_op jit(solution)/shard_map/while/body/eval_jaxpr/ppermute | solution.py:17
  450.7 12.1 %collective-permute-done = f32[8,128,128]{2,1,0:T(8,128)S(1)} collective-permute-done((f32[8,128,128]{2,1,0:T(8,128)S(1)}, f32[8,128,128]{2,1,0:T(8,128)S(1)}, u32[]{:S(2)}, u32[]{:S(2)}) %collective-permute-start) | collective-permute-done | bytes 524320 | tf_op jit(solution)/shard_map/while/body/eval_jaxpr/ppermute | solution.py:17
  464.9 11.2 %collective-permute-done = f32[8,128,128]{2,1,0:T(8,128)S(1)} collective-permute-done((f32[8,128,128]{2,1,0:T(8,128)S(1)}, f32[8,128,128]{2,1,0:T(8,128)S(1)}, u32[]{:S(2)}, u32[]{:S(2)}) %collective-permute-start) | collective-permute-done | bytes 524320 | tf_op jit(solution)/shard_map/while/body/eval_jaxpr/ppermute | solution.py:17
  477.1 2.6 multiply_reduce_fusion.1
  480.8 7.8 %fusion.62 = f32[256,4096]{1,0:T(8,128)} fusion(bf16[1024,4096]{1,0:T(8,128)(2,1)} %param.19, f32[32,8,8,128]{3,2,1,0:T(8,128)S(1)} %bitcast.132, f32[32,8,8,128]{3,2,1,0:T(8,128)S(1)} %bitcast.131, f32[1024]{0:T(1024)S(1)} %copy-done.10), kind=kOutput, calls=%fused_computation.66 | convolution fusion | flops 2148270080 | bytes 14684160 | tf_op jit(solution)/shard_map/dot_general | solution.py:117
  488.6 50.5 %reduce-scatter.2.cloned.1.call-done = f32[256,1024]{1,0:T(8,128)} async-done(((f32[256,4096]{1,0:T(8,128)}), f32[256,1024]{1,0:T(8,128)}) %reduce-scatter.2.cloned.1.call-update) | async-done | bytes 1048592 | tf_op jit(solution)/shard_map/reduce_scatter | solution.py:118
  539.1 2.1 convert_element_type.24
  (131 shorter events, 35.6 us)
Async XLA Ops:
  6.5 532.6 %reduce-scatter.2.cloned.1.call-start = ((), (), s32[]{:S(2)}) async-start(), calls=%async_computation.1 | async-start | bytes 5242880 | tf_op jit(solution)/shard_map/reduce_scatter | solution.py:118
  7.8 350.0 %collective-permute-start.1 = (s32[1]{0:T(128)}, s32[1]{0:T(128)}, u32[]{:S(2)}, u32[]{:S(2)}) collective-permute-start(s32[1]{0:T(128)} %slice.29), channel_id=1, source_target_pairs={{0,4},{4,8},{8,12},{12,16},{16,20},{20,24},{24,28},{1,5},{5,9},{9,... | collective-permute-start | bytes 20 | tf_op jit(solution)/shard_map/ppermute | solution.py:17
  16.3 0.9 copy-start.11
  17.2 4.0 copy-start.9
  21.6 1.1 copy-start.3
  25.4 2.8 copy-start.18
  25.4 3.0 copy-start.13
  25.4 3.0 copy-start.14
  25.4 3.0 copy-start.16
  350.8 7.0 %copy-start.19 = (s32[3]{0:T(128)S(1)}, s32[3]{0:T(128)}, u32[]{:S(2)}) copy-start(s32[3]{0:T(128)} %slice_reduce_fusion.1) | copy-start | bytes 40
  350.8 7.8 %copy-start.12 = (f32[8,4,128]{2,0,1:T(8,128)S(1)}, f32[8,4,128]{2,0,1:T(8,128)}, u32[]{:S(2)}) copy-start(f32[8,4,128]{2,0,1:T(8,128)} %copy-done.11) | copy-start | bytes 49156
  350.8 7.9 %copy-start.15 = (f32[8,4,128]{2,0,1:T(8,128)S(1)}, f32[8,4,128]{2,0,1:T(8,128)}, u32[]{:S(2)}) copy-start(f32[8,4,128]{2,0,1:T(8,128)} %copy.216) | copy-start | bytes 49156
  359.3 3.9 copy-start.6
  363.2 3.8 copy-start.17
  367.0 6.2 %copy-start.1 = (f32[8,4,128,256]{3,2,1,0:T(8,128)}, f32[8,4,128,256]{3,2,1,0:T(8,128)S(1)}, u32[]{:S(2)}) copy-start(f32[8,4,128,256]{3,2,1,0:T(8,128)S(1)} %fusion.11) | copy-start | bytes 12582916
  379.4 26.7 %copy-start.4 = (f32[32,8,8,128]{3,2,1,0:T(8,128)S(1)}, f32[32,8,8,128]{3,2,1,0:T(8,128)}, u32[]{:S(2)}) copy-start(f32[32,8,8,128]{3,2,1,0:T(8,128)} %copy-done.3) | copy-start | bytes 3145732
  406.1 4.3 copy-start.8
  406.1 6.5 %copy-start.5 = (f32[8,4,64,128]{3,2,1,0:T(8,128)S(1)}, f32[8,4,64,128]{3,2,1,0:T(8,128)}, u32[]{:S(2)}) copy-start(f32[8,4,64,128]{3,2,1,0:T(8,128)} %fusion.53) | copy-start | bytes 3145732
  410.4 2.2 copy-start.2
  412.6 2.1 copy-start.7
  418.2 15.3 %collective-permute-start = (f32[8,128,128]{2,1,0:T(8,128)S(1)}, f32[8,128,128]{2,1,0:T(8,128)S(1)}, u32[]{:S(2)}, u32[]{:S(2)}) collective-permute-start(f32[8,128,128]{2,1,0:T(8,128)S(1)} %get-tuple-element.333), channel_id=1, source_target_pairs={{0,4},{4,8},{8,12},{12,16},{16,20},{20,24},{24,28},{1,5},{5,9},{9,... | collective-permute-start | bytes 1572872 | tf_op jit(solution)/shard_map/while/body/eval_jaxpr/ppermute | solution.py:17
  433.5 0.8 copy-start
  434.3 14.3 %collective-permute-start = (f32[8,128,128]{2,1,0:T(8,128)S(1)}, f32[8,128,128]{2,1,0:T(8,128)S(1)}, u32[]{:S(2)}, u32[]{:S(2)}) collective-permute-start(f32[8,128,128]{2,1,0:T(8,128)S(1)} %get-tuple-element.333), channel_id=1, source_target_pairs={{0,4},{4,8},{8,12},{12,16},{16,20},{20,24},{24,28},{1,5},{5,9},{9,... | collective-permute-start | bytes 1572872 | tf_op jit(solution)/shard_map/while/body/eval_jaxpr/ppermute | solution.py:17
  448.6 0.8 copy-start
  449.4 13.4 %collective-permute-start = (f32[8,128,128]{2,1,0:T(8,128)S(1)}, f32[8,128,128]{2,1,0:T(8,128)S(1)}, u32[]{:S(2)}, u32[]{:S(2)}) collective-permute-start(f32[8,128,128]{2,1,0:T(8,128)S(1)} %get-tuple-element.333), channel_id=1, source_target_pairs={{0,4},{4,8},{8,12},{12,16},{16,20},{20,24},{24,28},{1,5},{5,9},{9,... | collective-permute-start | bytes 1572872 | tf_op jit(solution)/shard_map/while/body/eval_jaxpr/ppermute | solution.py:17
  462.8 0.8 copy-start
  463.6 12.5 %collective-permute-start = (f32[8,128,128]{2,1,0:T(8,128)S(1)}, f32[8,128,128]{2,1,0:T(8,128)S(1)}, u32[]{:S(2)}, u32[]{:S(2)}) collective-permute-start(f32[8,128,128]{2,1,0:T(8,128)S(1)} %get-tuple-element.333), channel_id=1, source_target_pairs={{0,4},{4,8},{8,12},{12,16},{16,20},{20,24},{24,28},{1,5},{5,9},{9,... | collective-permute-start | bytes 1572872 | tf_op jit(solution)/shard_map/while/body/eval_jaxpr/ppermute | solution.py:17
  476.1 0.8 copy-start
  479.7 1.1 copy-start.10
Sparse Core Ops, SparseCore 0:
  488.8 50.2 reduce-scatter.1
where the time goes:
time: 551 us; the launch traced here: 548 us
  other arithmetic  332 us (60%)
  waiting for transfers between devices  101 us (18%)
  matrix products  70.7 us (13%)
  local copies, waits for them, and re-layouts  23.7 us (4%)
  between operations  13.9 us (3%)
  starting transfers between devices  6.41 us (1%)
    another operation x4, other arithmetic, shards(): lax.linalg.triangular_solve(system, right_side, left_side=True, lower=Tru...  317 us
    reduce_scatter x1, waiting for transfers between devices, shards(): lax.psum_scatter(terms, 'head', scatter_dimension=1, tiled=True)  50.5 us
    ppermute x5, waiting for transfers between devices, shifted(): lax.ppermute(value, axis, [(source, source + steps) for source in range(i...  50.3 us
  transfers between devices with their start and end apart: 6, of which 5 were waited for; matrix products, arithmetic and copies ran while one was open for 63% of the time, Pallas kernels for 0%

commit v1 on v0

v1 whole, which is shorter than its diff:
```python
import functools
import jax
import jax.numpy as jnp
from jax import lax
from jax.experimental import pallas as pl
from jax.experimental.pallas import tpu as pltpu
from jax.sharding import PartitionSpec as P

DK = 128
DV = 128
GROUP = 64
ROWS = 2 * GROUP
HEADS_STEP = 2
F32 = jnp.float32
BF16 = jnp.bfloat16


def halves(a):
    if a.dtype == BF16:
        return a, None
    hi = a.astype(BF16)
    return hi, (a - hi.astype(F32)).astype(BF16)


def one(a, b):
    return jnp.dot(a, b, preferred_element_type=F32)


def mul(a, b):
    a_hi, a_lo = a if isinstance(a, tuple) else halves(a)
    b_hi, b_lo = b if isinstance(b, tuple) else halves(b)
    out = one(a_hi, b_hi)
    if a_lo is not None:
        out = out + one(a_lo, b_hi)
    if b_lo is not None:
        out = out + one(a_hi, b_lo)
    return out


def exact(a, b):
    return lax.dot_general(
        a, b, (((1,), (0,)), ((), ())), precision=lax.Precision.HIGHEST, preferred_element_type=F32
    )


def local_kernel(q_ref, k_ref, v_ref, beta_ref, log_ref, seg_ref, map_ref, add_ref, mapped_ref, local_ref):
    step = pl.program_id(0)
    blocks = q_ref.shape[0] // GROUP
    row = lax.broadcasted_iota(jnp.int32, (ROWS, ROWS), 0)
    col = lax.broadcasted_iota(jnp.int32, (ROWS, ROWS), 1)
    row_tok = lax.broadcasted_iota(jnp.int32, (GROUP, ROWS), 0)
    col_tok = lax.broadcasted_iota(jnp.int32, (GROUP, ROWS), 1)
    eye = (row == col).astype(F32)
    summing = ((row < GROUP) & (row <= col // 2)).astype(F32)
    spreading = ((row < GROUP) & (row == col // 2)).astype(F32)
    weaving = jnp.where(
        row < GROUP, (col == 2 * row).astype(F32), (col == 2 * (row - GROUP) + 1).astype(F32)
    )
    units = []
    for which in range(HEADS_STEP):
        head = step * HEADS_STEP + which
        logs = log_ref[pl.ds(head, 1), :]
        first = beta_ref[0, pl.ds(head, 1), :]
        second = beta_ref[1, pl.ds(head, 1), :]
        segs = seg_ref[...].astype(F32)
        for block in range(blocks):
            units.append((which, block, logs, first, second, segs))

    prepared = []
    for which, block, logs, first, second, segs in units:
        toks = slice(block * GROUP, (block + 1) * GROUP)
        zero = jnp.zeros((1, GROUP), F32)
        packed = jnp.concatenate(
            [
                jnp.concatenate([logs[:, toks], zero], axis=1),
                jnp.concatenate([first[:, toks], second[:, toks]], axis=1),
                jnp.concatenate([segs[:, toks], zero], axis=1),
                jnp.zeros((5, ROWS), F32),
            ],
            axis=0,
        )
        cum_row = exact(packed, summing)[0:1]
        beta_row = exact(packed, weaving)[1:2]
        seg_row = exact(packed, spreading)[2:3]
        columns = jnp.transpose(
            jnp.concatenate([cum_row, beta_row, seg_row, jnp.zeros((ROWS - 3, ROWS), F32)], axis=0)
        )
        cum_col, beta_col, seg_col = columns[:, 0:1], columns[:, 1:2], columns[:, 2:3]
        tok_columns = jnp.transpose(
            jnp.concatenate(
                [
                    exact(packed, ((row < GROUP) & (row <= col)).astype(F32))[0:1],
                    packed[2:3],
                    jnp.zeros((ROWS - 2, ROWS), F32),
                ],
                axis=0,
            )
        )[:GROUP]
        cum_tok, seg_tok = tok_columns[:, 0:1], tok_columns[:, 1:2]
        start = segs[:, 0:1] if block == 0 else segs[:, block * GROUP - 1 : block * GROUP]
        last_seg = segs[:, (block + 1) * GROUP - 1 : (block + 1) * GROUP]
        cum_last = cum_row[:, ROWS - 1 : ROWS]

        lanes = slice(which * DK, (which + 1) * DK)
        keys = k_ref[block * ROWS : (block + 1) * ROWS, lanes]
        query = q_ref[toks, lanes]
        keys_t = jnp.transpose(keys.astype(F32)).astype(BF16)
        both = one(jnp.concatenate([keys, query], axis=0), keys_t)
        gram, meets = both[:ROWS], both[ROWS:]
        diagonal = gram * eye
        inv_row = lax.rsqrt(jnp.sum(diagonal, axis=0, keepdims=True) + 1e-06)
        inv_col = lax.rsqrt(jnp.sum(diagonal, axis=1, keepdims=True) + 1e-06)
        query_f = query.astype(F32)
        inv_query = lax.rsqrt(jnp.sum(query_f * query_f, axis=1, keepdims=True) + 1e-06)
        lower = jnp.where(
            (seg_col == seg_row) & (row > col),
            (beta_col * inv_col) * jnp.exp(cum_col - cum_row) * (gram * inv_row),
            0.0,
        )
        scores = jnp.where(
            (seg_tok == seg_row) & (col_tok <= 2 * row_tok + 1),
            inv_query * jnp.exp(cum_tok - cum_row) * (meets * inv_row),
            0.0,
        )
        entry_row = jnp.where(seg_row == start, jnp.exp(cum_row), 0.0)
        entry_tok = jnp.where(seg_tok == start, jnp.exp(cum_tok), 0.0)
        tail_col = jnp.where(seg_col == last_seg, jnp.exp(cum_last - cum_col), 0.0)
        tail_entry = jnp.where(last_seg == start, jnp.exp(cum_last), 0.0)
        prepared.append(
            dict(
                keys=keys,
                keys_t=keys_t,
                lower=lower,
                scores=scores,
                value_scale=beta_row,
                key_scale=beta_row * entry_row * inv_row,
                tail=tail_col * inv_col,
                tail_entry=tail_entry,
                reach=(entry_tok * inv_query) * query_f,
            )
        )

    inverses = [eye - jnp.where(row // 2 == col // 2, p["lower"], 0.0) for p in prepared]
    size = 2
    while size < ROWS:
        below = (row // (2 * size) == col // (2 * size)) & (row // size > col // size)
        split = [halves(x) for x in inverses]
        inner = [mul(jnp.where(below, p["lower"], 0.0), s) for p, s in zip(prepared, split)]
        inverses = [x - mul(s, i) for x, s, i in zip(inverses, split, inner)]
        size *= 2

    solved = []
    for (which, block, *_), p, x in zip(units, prepared, inverses):
        values = v_ref[block * ROWS : (block + 1) * ROWS, which * DV : (which + 1) * DV]
        key_mix = mul(x * p["key_scale"], p["keys"])
        pseudo = mul(x * p["value_scale"], values)
        solved.append(jnp.concatenate([key_mix, pseudo], axis=1))
    reads = [mul(p["scores"], s) for p, s in zip(prepared, solved)]
    moves = [mul(p["keys_t"], s * p["tail"]) for p, s in zip(prepared, solved)]
    running = [None] * HEADS_STEP
    for block in range(blocks):
        for which in range(HEADS_STEP):
            at = which * blocks + block
            p, toks = prepared[at], slice(block * GROUP, (block + 1) * GROUP)
            reach = p["reach"] - reads[at][:, :DK]
            block_map = p["tail_entry"] * eye - moves[at][:, :DK]
            if block == 0:
                mapped, local = reach, reads[at][:, DK:]
                running[which] = jnp.concatenate([block_map, moves[at][:, DK:]], axis=1)
            else:
                before = halves(running[which])
                out = mul(reach, before)
                mapped, local = out[:, :DK], out[:, DK:] + reads[at][:, DK:]
                turned = mul(block_map, before)
                running[which] = jnp.concatenate(
                    [turned[:, :DK], turned[:, DK:] + moves[at][:, DK:]], axis=1
                )
            mapped_ref[which, toks, :] = mapped
            local_ref[which, toks, :] = local
    for which in range(HEADS_STEP):
        map_ref[which] = running[which][:, :DK]
        add_ref[which] = running[which][:, DK:]


def local_parts(queries, keys, values, betas, log_decay, segment):
    tok_local = queries.shape[0]
    heads_local = betas.shape[1]
    lanes = HEADS_STEP * DK
    whole = lambda *shape: pl.BlockSpec(shape, lambda h: (0,) * len(shape))
    per_head = lambda rows: pl.BlockSpec((HEADS_STEP, rows, DK), lambda h: (h, 0, 0))
    shape = lambda rows: jax.ShapeDtypeStruct((heads_local, rows, DK), F32)
    return pl.pallas_call(
        local_kernel,
        grid=(heads_local // HEADS_STEP,),
        in_specs=[
            pl.BlockSpec((tok_local, lanes), lambda h: (0, h)),
            pl.BlockSpec((2 * tok_local, lanes), lambda h: (0, h)),
            pl.BlockSpec((2 * tok_local, lanes), lambda h: (0, h)),
            whole(2, heads_local, tok_local),
            whole(heads_local, tok_local),
            whole(1, tok_local),
        ],
        out_specs=[per_head(DK), per_head(DK), per_head(tok_local), per_head(tok_local)],
        out_shape=[shape(DK), shape(DK), shape(tok_local), shape(tok_local)],
        compiler_params=pltpu.CompilerParams(vmem_limit_bytes=48 * 1024 * 1024),
        cost_estimate=pl.CostEstimate(flops=12 * 10**9, bytes_accessed=8 * 10**6, transcendentals=10**6),
        name="local_blocks",
    )(
        queries,
        keys.reshape(2 * tok_local, -1),
        values.reshape(2 * tok_local, -1),
        betas,
        log_decay,
        segment.reshape(1, tok_local),
    )


def shifted(value, axis, steps):
    count = lax.axis_size(axis)
    return lax.ppermute(value, axis, [(source, source + steps) for source in range(count - steps)])


def shards(queries, keys, values, betas, log_decay, segment, gain, out_weight):
    tok_local = queries.shape[0]
    heads_local = betas.shape[1]
    before = shifted(segment[tok_local - 1 :], "ctx", 1)
    maps, adds, mapped, local_out = local_parts(queries, keys, values, betas, log_decay, segment)
    linked = ((before[0] == segment[0]) & (lax.axis_index("ctx") > 0)).astype(F32)
    turns = min(8, lax.axis_size("ctx") // 2)
    arrived = None
    leaving = adds
    for _ in range(turns):
        arrived = shifted(leaving, "ctx", 1) * linked
        leaving = jnp.einsum("hab,hbv->hav", maps, arrived, precision=lax.Precision.HIGH) + adds
    attended = local_out + jnp.einsum(
        "hik,hkv->hiv", mapped, arrived, precision=lax.Precision.HIGH
    )
    attended = jnp.transpose(attended, (1, 0, 2))
    inverse_rms = 1.0 / jnp.sqrt(jnp.mean(attended * attended, axis=-1, keepdims=True) + 1e-06)
    normed = ((attended * inverse_rms).reshape(tok_local, heads_local * DV) * gain[None, :]).astype(BF16)
    terms = jnp.dot(normed, out_weight, preferred_element_type=F32)
    return lax.psum_scatter(terms, "head", scatter_dimension=1, tiled=True).astype(BF16)


def solution(mesh):
    return jax.shard_map(
        shards,
        mesh=mesh,
        in_specs=(
            P("ctx", "head"),
            P("ctx", None, "head"),
            P("ctx", None, "head"),
            P(None, "head", "ctx"),
            P("head", "ctx"),
            P("ctx"),
            P("head"),
            P("head", None),
        ),
        out_specs=P("ctx", "head"),
        check_vma=False,
    )
```

time: 551 us -> 170 us (0.31)
  other arithmetic: 332 us -> 2.64 us
  matrix products: 70.7 us -> 11.2 us
  Pallas kernels: 0 us -> 25.6 us
  local copies, waits for them, and re-layouts: 23.7 us -> 8.97 us
    another operation x7 -> x0, other arithmetic: 318 us -> none  [the longest x4 317 us: shards(): lax.linalg.triangular_solve(system, right_side, left_side=True, lower=Tru...]
    dot_general x22 -> x5, matrix products: 67 us -> 11.2 us  [the longest x1 7.72 us: shards(): terms = jnp.dot(normed, out_weight, preferred_element_type=F32)]
    pallas_call x0 -> x1, Pallas kernels: none -> 25.6 us  [local_parts(): pl.pallas_call(local_kernel, grid=(heads_local // HEADS_STEP,), in_specs=...]
  transfers between devices with their start and end apart: 6 -> 6, of which waited for: 5 -> 5; matrix products, arithmetic and copies ran while one was open for 63% -> 0% of each run, Pallas kernels for 0% -> 0%
where the time goes in v1:
time: 170 us; the launch traced here: 167 us
  waiting for transfers between devices  97.5 us (57%)
  Pallas kernels  25.6 us (15%)
  between operations  14.8 us (9%)
  matrix products  11.2 us (7%)
  local copies, waits for them, and re-layouts  8.97 us (5%)
  starting transfers between devices  6.75 us (4%)
  other arithmetic  2.64 us (2%)
    reduce_scatter x1, waiting for transfers between devices, shards(): lax.psum_scatter(terms, 'head', scatter_dimension=1, tiled=True)  50.3 us
    ppermute x5, waiting for transfers between devices, shifted(): lax.ppermute(value, axis, [(source, source + steps) for source in range(c...  47.2 us
    pallas_call x1, Pallas kernels, local_parts(): pl.pallas_call(local_kernel, grid=(heads_local // HEADS_STEP,), in_specs=...  25.6 us
    dot_general x1, matrix products, shards(): terms = jnp.dot(normed, out_weight, preferred_element_type=F32)  7.72 us
    ppermute x5, starting transfers between devices, shifted(): lax.ppermute(value, axis, [(source, source + steps) for source in range(c...  6.75 us
    unnamed x14, local copies, waits for them, and re-layouts  5.1 us
  transfers between devices with their start and end apart: 6, of which 5 were waited for; matrix products, arithmetic and copies ran while one was open for 0% of the time, Pallas kernels for 0%

profile of v1, /device:TPU:27, one launch (start us, length us, event | category | flops | bytes accessed | tf_op | source)
XLA Modules:
  0.0 167.4 jit_solution(18428059774984302044)
XLA Ops:
  6.5 1.5 reshape.23.k_ref
  8.0 1.5 reshape.24.v_ref
  9.5 0.0 copy-start.2
  9.5 0.7 copy-done.2
  10.2 1.0 copy-done.3
  11.2 0.7 copy-done.4
  11.9 0.7 copy-done.5
  12.6 25.6 %local_blocks.1 = (f32[8,128,128]{2,1,0:T(8,128)S(1)}, f32[8,128,128]{2,1,0:T(8,128)S(1)}, f32[8,256,128]{2,1,0:T(8,128)S(1)}, f32[8,256,128]{2,1,0:T(8,128)S(1)}) custom-call(bf16[256,1024]{1,0:T(8,128)(2,1)S(1)} %copy-done.3, bf16[512,1024]{1,0:T(8,128)(2,1)S(1)} %reshape.23.k_ref, bf16[512,1024]{1,0:T(8,128)(2,1)S(1)} %reshape.24.v_ref, ...), custom_call_target="tpu_custom_call" | custom-call | flops 12000000000 | bytes 8000000 | tf_op jit(solution)/shard_map/local_blocks/pallas_call | solution.py:192
  38.3 1.0 copy-done
  39.3 1.0 copy-done.1
  40.3 1.4 collective-permute-start
  41.7 0.6 fusion.10
  42.3 1.3 collective-permute-start.1
  43.6 11.5 %collective-permute-done.1 = s32[1]{0:T(128)} collective-permute-done((s32[1]{0:T(128)}, s32[1]{0:T(128)}, u32[]{:S(2)}, u32[]{:S(2)}) %collective-permute-start.1) | collective-permute-done | bytes 36 | tf_op jit(solution)/shard_map/ppermute | solution.py:220
  56.3 0.0 collective-permute-done
  56.3 0.4 convolution_add_fusion.3
  56.7 1.3 collective-permute-start.2
  58.0 12.3 %collective-permute-done.2 = f32[8,128,128]{2,1,0:T(8,128)S(1)} collective-permute-done((f32[8,128,128]{2,1,0:T(8,128)S(1)}, f32[8,128,128]{2,1,0:T(8,128)S(1)}, u32[]{:S(2)}, u32[]{:S(2)}) %collective-permute-start.2) | collective-permute-done | bytes 524320 | tf_op jit(solution)/shard_map/ppermute | solution.py:220
  70.2 0.4 convolution_add_fusion.2
  70.6 1.3 collective-permute-start.3
  71.9 12.2 %collective-permute-done.3 = f32[8,128,128]{2,1,0:T(8,128)S(1)} collective-permute-done((f32[8,128,128]{2,1,0:T(8,128)S(1)}, f32[8,128,128]{2,1,0:T(8,128)S(1)}, u32[]{:S(2)}, u32[]{:S(2)}) %collective-permute-start.3) | collective-permute-done | bytes 524320 | tf_op jit(solution)/shard_map/ppermute | solution.py:220
  84.2 0.4 convolution_add_fusion.1
  84.5 1.5 collective-permute-start.4
  86.0 11.2 %collective-permute-done.4 = f32[8,128,128]{2,1,0:T(8,128)S(1)} collective-permute-done((f32[8,128,128]{2,1,0:T(8,128)S(1)}, f32[8,128,128]{2,1,0:T(8,128)S(1)}, u32[]{:S(2)}, u32[]{:S(2)}) %collective-permute-start.4) | collective-permute-done | bytes 524320 | tf_op jit(solution)/shard_map/ppermute | solution.py:220
  97.2 2.4 %multiply_reduce_fusion = (f32[256,8]{0,1:T(8,128)S(1)}, f32[256,8,128]{2,0,1:T(8,128)S(1)}) fusion(f32[8,256,128]{2,1,0:T(8,128)} %copy-done.1, f32[8,256,128]{2,1,0:T(8,128)} %copy-done, f32[8,128,128]{2,1,0:T(8,128)S(1)} %collective-permute-done.4, f32[]{:T(128)S(6)} %convert_element_type.9), kind=kOutput, calls=%fused_computation.7 | convolution fusion | flops 202242048 | bytes 3678212 | tf_op jit(solution)/shard_map/hik,hkv->hiv/dot_general | solution.py:235
  99.6 0.3 broadcast_multiply_fusion
  99.9 0.3 copy.13
  100.3 0.2 fusion.1
  100.5 7.7 %fusion.11 = f32[256,4096]{1,0:T(8,128)} fusion(bf16[256,1024]{0,1:T(8,128)(2,1)S(1)} %fusion.1, bf16[1024,4096]{1,0:T(8,128)(2,1)} %param.15), kind=kOutput, calls=%fused_computation.19 | convolution fusion | flops 2147483648 | bytes 13107200 | tf_op jit(solution)/shard_map/dot_general | solution.py:241
  108.2 0.0 reduce-scatter.2.cloned.1.call-update
  108.2 50.3 %reduce-scatter.2.cloned.1.call-done = f32[256,1024]{1,0:T(8,128)} async-done(((f32[256,4096]{1,0:T(8,128)}), f32[256,1024]{1,0:T(8,128)}) %reduce-scatter.2.cloned.1.call-update) | async-done | bytes 1048592 | tf_op jit(solution)/shard_map/reduce_scatter | solution.py:242
  158.5 2.1 %convert_element_type.11 = bf16[256,1024]{1,0:T(8,128)(2,1)} convert(f32[256,1024]{1,0:T(8,128)} %reduce-scatter.2.cloned.1.call-done) | non-fusion elementwise | flops 262144 | bytes 1572864 | tf_op jit(solution)/shard_map/convert_element_type | solution.py:242
  (9 shorter events, 0.0 us)
Async XLA Ops:
  6.5 152.0 %reduce-scatter.2.cloned.1.call-start = ((), (), s32[]{:S(2)}) async-start(), calls=%async_computation.1 | async-start | bytes 5242880 | tf_op jit(solution)/shard_map/reduce_scatter | solution.py:242
  9.5 0.7 copy-start.2
  10.2 1.0 copy-start.3
  11.2 0.7 copy-start.4
  11.9 0.7 copy-start.5
  38.3 1.0 copy-start
  39.3 1.0 copy-start.1
  40.3 60.0 %copy-start.6 = (f32[1024]{0:T(1024)S(1)}, f32[1024]{0:T(1024)}, u32[]{:S(2)}) copy-start(f32[1024]{0:T(1024)} %param.14) | copy-start | bytes 12292
  40.3 16.0 %collective-permute-start = (f32[8,128,128]{2,1,0:T(8,128)S(1)}, f32[8,128,128]{2,1,0:T(8,128)S(1)}, u32[]{:S(2)}, u32[]{:S(2)}) collective-permute-start(f32[8,128,128]{2,1,0:T(8,128)S(1)} %get-tuple-element.12), channel_id=1, source_target_pairs={{0,4},{4,8},{8,12},{12,16},{16,20},{20,24},{24,28},{1,5},{5,9},{9,... | collective-permute-start | bytes 1572872 | tf_op jit(solution)/shard_map/ppermute | solution.py:220
  42.3 12.8 %collective-permute-start.1 = (s32[1]{0:T(128)}, s32[1]{0:T(128)}, u32[]{:S(2)}, u32[]{:S(2)}) collective-permute-start(s32[1]{0:T(128)} %get-tuple-element.14), channel_id=1, source_target_pairs={{0,4},{4,8},{8,12},{12,16},{16,20},{20,24},{24,28},{1,5},{5,9},{9,... | collective-permute-start | bytes 20 | tf_op jit(solution)/shard_map/ppermute | solution.py:220
  56.7 13.6 %collective-permute-start.2 = (f32[8,128,128]{2,1,0:T(8,128)S(1)}, f32[8,128,128]{2,1,0:T(8,128)S(1)}, u32[]{:S(2)}, u32[]{:S(2)}) collective-permute-start(f32[8,128,128]{2,1,0:T(8,128)S(1)} %convolution_add_fusion.3), channel_id=1, source_target_pairs={{0,4},{4,8},{8,12},{12,16},{16,20},{20,24},{24,28},{1,5},{5,9},{9,... | collective-permute-start | bytes 1572872 | tf_op jit(solution)/shard_map/ppermute | solution.py:220
  70.6 13.5 %collective-permute-start.3 = (f32[8,128,128]{2,1,0:T(8,128)S(1)}, f32[8,128,128]{2,1,0:T(8,128)S(1)}, u32[]{:S(2)}, u32[]{:S(2)}) collective-permute-start(f32[8,128,128]{2,1,0:T(8,128)S(1)} %convolution_add_fusion.2), channel_id=1, source_target_pairs={{0,4},{4,8},{8,12},{12,16},{16,20},{20,24},{24,28},{1,5},{5,9},{9,... | collective-permute-start | bytes 1572872 | tf_op jit(solution)/shard_map/ppermute | solution.py:220
  84.5 12.6 %collective-permute-start.4 = (f32[8,128,128]{2,1,0:T(8,128)S(1)}, f32[8,128,128]{2,1,0:T(8,128)S(1)}, u32[]{:S(2)}, u32[]{:S(2)}) collective-permute-start(f32[8,128,128]{2,1,0:T(8,128)S(1)} %convolution_add_fusion.1), channel_id=1, source_target_pairs={{0,4},{4,8},{8,12},{12,16},{16,20},{20,24},{24,28},{1,5},{5,9},{9,... | collective-permute-start | bytes 1572872 | tf_op jit(solution)/shard_map/ppermute | solution.py:220
Sparse Core Ops, SparseCore 0:
  108.4 50.0 reduce-scatter.1

commit v2 on v1

--- a/solution.py
+++ b/solution.py
@@ -43,7 +43,9 @@
     )
 
 
-def local_kernel(q_ref, k_ref, v_ref, beta_ref, log_ref, seg_ref, map_ref, add_ref, mapped_ref, local_ref):
+def local_kernel(
+    q_ref, k_ref, v_ref, beta_ref, log_ref, seg_ref, map_ref, add_ref, mapped_ref, local_ref, edge_ref
+):
     step = pl.program_id(0)
     blocks = q_ref.shape[0] // GROUP
     row = lax.broadcasted_iota(jnp.int32, (ROWS, ROWS), 0)
@@ -180,6 +182,9 @@
     for which in range(HEADS_STEP):
         map_ref[which] = running[which][:, :DK]
         add_ref[which] = running[which][:, DK:]
+    segs = seg_ref[...].astype(F32)
+    edge_ref[0] = jnp.broadcast_to(segs[:, 0:1], (8, 128))
+    edge_ref[1] = jnp.broadcast_to(segs[:, segs.shape[1] - 1 :], (8, 128))
 
 
 def local_parts(queries, keys, values, betas, log_decay, segment):
@@ -200,8 +205,9 @@
             whole(heads_local, tok_local),
             whole(1, tok_local),
         ],
-        out_specs=[per_head(DK), per_head(DK), per_head(tok_local), per_head(tok_local)],
-        out_shape=[shape(DK), shape(DK), shape(tok_local), shape(tok_local)],
+        out_specs=[per_head(DK), per_head(DK), per_head(tok_local), per_head(tok_local), whole(2, 8, 128)],
+        out_shape=[shape(DK), shape(DK), shape(tok_local), shape(tok_local)]
+        + [jax.ShapeDtypeStruct((2, 8, 128), F32)],
         compiler_params=pltpu.CompilerParams(vmem_limit_bytes=48 * 1024 * 1024),
         cost_estimate=pl.CostEstimate(flops=12 * 10**9, bytes_accessed=8 * 10**6, transcendentals=10**6),
         name="local_blocks",
@@ -215,31 +221,202 @@
     )
 
 
-def shifted(value, axis, steps):
-    count = lax.axis_size(axis)
-    return lax.ppermute(value, axis, [(source, source + steps) for source in range(count - steps)])
+MESH = pl.DeviceIdType.MESH
+CHUNK = 256
+
+
+def finish_kernel(
+    map_ref, add_ref, mapped_ref, local_ref, edge_ref, gain_ref, weight_ref, out_ref,
+    weight, normed, states, leaving, seg_in, outgoing, incoming, total, summed,
+    weight_sem, seg_send, seg_recv, chain_send, chain_recv, pair_send, pair_recv, far_send, far_recv,
+):
+    place, places = lax.axis_index("ctx"), lax.axis_size("ctx")
+    mine = lax.axis_index("head")
+    heads = map_ref.shape[0]
+    width = out_ref.shape[1]
+    chunks = width // CHUNK
+    beside = mine + 1 - 2 * lax.rem(mine, 2)
+    across = lax.rem(mine + 2, 4)
+    diagonal = 3 - mine
+    after, before = place + 1, place - 1
+    has_after, has_before = place < places - 1, place > 0
+
+    fetch = pltpu.make_async_copy(weight_ref, weight, weight_sem)
+    fetch.start()
+    barrier = pltpu.get_barrier_semaphore()
+    for partner in (beside, across):
+        pl.semaphore_signal(barrier, inc=1, device_id=(place, partner), device_id_type=MESH)
+
+    @pl.when(has_after)
+    def _():
+        pl.semaphore_signal(barrier, inc=1, device_id=(after, mine), device_id_type=MESH)
+
+    @pl.when(has_before)
+    def _():
+        pl.semaphore_signal(barrier, inc=1, device_id=(before, mine), device_id_type=MESH)
+
+    pl.semaphore_wait(barrier, 2 + has_after.astype(jnp.int32) + has_before.astype(jnp.int32))
+
+    seg_copy = pltpu.make_async_remote_copy(
+        src_ref=edge_ref.at[1], dst_ref=seg_in, send_sem=seg_send, recv_sem=seg_recv,
+        device_id=(after, mine), device_id_type=MESH,
+    )
+
+    def state_copy(head):
+        return pltpu.make_async_remote_copy(
+            src_ref=leaving.at[head], dst_ref=states.at[head],
+            send_sem=chain_send.at[head], recv_sem=chain_recv.at[head],
+            device_id=(after, mine), device_id_type=MESH,
+        )
+
+    def attend(head, state):
+        attended = local_ref[head]
+        if state is not None:
+            attended = attended + mul(mapped_ref[head], state)
+        inverse_rms = 1.0 / jnp.sqrt(jnp.mean(attended * attended, axis=-1, keepdims=True) + 1e-06)
+        lanes = pl.ds(pl.multiple_of(head * DV, DV), DV)
+        normed[:, lanes] = (attended * inverse_rms * gain_ref[:, lanes]).astype(BF16)
+
+    @pl.when(place == 0)
+    def _():
+        seg_copy.start()
+
+        def first(head, carry):
+            leaving[head] = add_ref[head]
+            state_copy(head).start()
+            return carry
+
+        lax.fori_loop(0, heads, first, 0)
+
+        def read(head, carry):
+            attend(head, None)
+            return carry
+
+        lax.fori_loop(0, heads, read, 0)
+
+    @pl.when(has_before)
+    def _():
+        @pl.when(has_after)
+        def _():
+            seg_copy.start()
+
+        seg_copy.wait_recv()
+        linked = seg_in[0:1, :] == edge_ref[0, 0:1, :]
+
+        def link(head, carry):
+            state_copy(head).wait_recv()
+            state = halves(jnp.where(linked, states[head], 0.0))
+
+            @pl.when(has_after)
+            def _():
+                leaving[head] = mul(map_ref[head], state) + add_ref[head]
+                state_copy(head).start()
+
+            attend(head, state)
+            return carry
+
+        lax.fori_loop(0, heads, link, 0)
+
+    fetch.wait()
+
+    def product(owner, chunk):
+        lanes = pl.ds(pl.multiple_of(owner * width + chunk * CHUNK, CHUNK), CHUNK)
+        return one(normed[...], weight[:, lanes])
+
+    def pair_copy(near, chunk):
+        return pltpu.make_async_remote_copy(
+            src_ref=outgoing.at[near, chunk], dst_ref=incoming.at[near, chunk],
+            send_sem=pair_send.at[near, chunk], recv_sem=pair_recv.at[near, chunk],
+            device_id=(place, beside), device_id_type=MESH,
+        )
+
+    def far_copy(chunk):
+        return pltpu.make_async_remote_copy(
+            src_ref=total.at[0, chunk], dst_ref=summed.at[chunk],
+            send_sem=far_send.at[chunk], recv_sem=far_recv.at[chunk],
+            device_id=(place, across), device_id_type=MESH,
+        )
+
+    for near, theirs, ours in ((0, diagonal, across), (1, beside, mine)):
+
+        def give(chunk, carry):
+            outgoing[near, chunk] = product(theirs, chunk)
+            pair_copy(near, chunk).start()
+            return carry
+
+        def take(chunk, carry):
+            part = product(ours, chunk)
+            pair_copy(near, chunk).wait_recv()
+            total[near, chunk] = part + incoming[near, chunk]
+            if near == 0:
+                far_copy(chunk).start()
+            return carry
+
+        lax.fori_loop(0, chunks, give, 0)
+        lax.fori_loop(0, chunks, take, 0)
+
+    for chunk in range(chunks):
+        far_copy(chunk).wait_recv()
+        out_ref[:, chunk * CHUNK : (chunk + 1) * CHUNK] = (total[1, chunk] + summed[chunk]).astype(BF16)
+
+    for chunk in range(chunks):
+        far_copy(chunk).wait_send()
+        for near in range(2):
+            pair_copy(near, chunk).wait_send()
+
+    @pl.when(has_after)
+    def _():
+        seg_copy.wait_send()
+
+        def sent(head, carry):
+            state_copy(head).wait_send()
+            return carry
+
+        lax.fori_loop(0, heads, sent, 0)
+
+
+def finish(maps, adds, mapped, local_out, edges, gain, out_weight):
+    heads, tok_local = mapped.shape[:2]
+    width = out_weight.shape[1] // lax.axis_size("head")
+    chunks = width // CHUNK
+    dma = pltpu.SemaphoreType.DMA
+    vmem = pl.BlockSpec(memory_space=pltpu.VMEM)
+    return pl.pallas_call(
+        finish_kernel,
+        out_shape=jax.ShapeDtypeStruct((tok_local, width), BF16),
+        in_specs=[vmem] * 6 + [pl.BlockSpec(memory_space=pl.ANY)],
+        out_specs=vmem,
+        scratch_shapes=[
+            pltpu.VMEM(out_weight.shape, BF16),
+            pltpu.VMEM((tok_local, heads * DV), BF16),
+            pltpu.VMEM((heads, DK, DV), F32),
+            pltpu.VMEM((heads, DK, DV), F32),
+            pltpu.VMEM((8, 128), F32),
+            pltpu.VMEM((2, chunks, tok_local, CHUNK), F32),
+            pltpu.VMEM((2, chunks, tok_local, CHUNK), F32),
+            pltpu.VMEM((2, chunks, tok_local, CHUNK), F32),
+            pltpu.VMEM((chunks, tok_local, CHUNK), F32),
+            dma,
+            dma,
+            dma,
+            dma((heads,)),
+            dma((heads,)),
+            dma((2, chunks)),
+            dma((2, chunks)),
+            dma((chunks,)),
+            dma((chunks,)),
+        ],
+        compiler_params=pltpu.CompilerParams(
+            vmem_limit_bytes=48 * 1024 * 1024, collective_id=0, has_side_effects=True
+        ),
+        cost_estimate=pl.CostEstimate(flops=4 * 10**9, bytes_accessed=14 * 10**6, transcendentals=10**4),
+        name="chain_and_project",
+    )(maps, adds, mapped, local_out, edges, gain, out_weight)
 
 
 def shards(queries, keys, values, betas, log_decay, segment, gain, out_weight):
-    tok_local = queries.shape[0]
-    heads_local = betas.shape[1]
-    before = shifted(segment[tok_local - 1 :], "ctx", 1)
-    maps, adds, mapped, local_out = local_parts(queries, keys, values, betas, log_decay, segment)
-    linked = ((before[0] == segment[0]) & (lax.axis_index("ctx") > 0)).astype(F32)
-    turns = min(8, lax.axis_size("ctx") // 2)
-    arrived = None
-    leaving = adds
-    for _ in range(turns):
-        arrived = shifted(leaving, "ctx", 1) * linked
-        leaving = jnp.einsum("hab,hbv->hav", maps, arrived, precision=lax.Precision.HIGH) + adds
-    attended = local_out + jnp.einsum(
-        "hik,hkv->hiv", mapped, arrived, precision=lax.Precision.HIGH
-    )
-    attended = jnp.transpose(attended, (1, 0, 2))
-    inverse_rms = 1.0 / jnp.sqrt(jnp.mean(attended * attended, axis=-1, keepdims=True) + 1e-06)
-    normed = ((attended * inverse_rms).reshape(tok_local, heads_local * DV) * gain[None, :]).astype(BF16)
-    terms = jnp.dot(normed, out_weight, preferred_element_type=F32)
-    return lax.psum_scatter(terms, "head", scatter_dimension=1, tiled=True).astype(BF16)
+    parts = local_parts(queries, keys, values, betas, log_decay, segment)
+    return finish(*parts, gain.reshape(1, -1), out_weight)
 
 
 def solution(mesh):

time: 170 us -> 95.2 us (0.56); the launches traced: 167 us -> 94.8 us
  waiting for transfers between devices: 97.5 us -> 0 us
  Pallas kernels: 25.6 us -> 87.9 us
  between operations: 14.8 us -> 0.05 us
  matrix products: 11.2 us -> 0 us
  starting transfers between devices: 6.75 us -> 0 us
  other arithmetic: 2.64 us -> 0 us
  local copies, waits for them, and re-layouts: 8.97 us -> 6.86 us
    pallas_call x0 -> x1, Pallas kernels: none -> 62.3 us  [finish(): pl.pallas_call(finish_kernel, out_shape=jax.ShapeDtypeStruct((tok_local,...]
    reduce_scatter x1 -> x0, waiting for transfers between devices: 50.3 us -> none  [shards(): lax.psum_scatter(terms, 'head', scatter_dimension=1, tiled=True)]
    ppermute x5 -> x0, waiting for transfers between devices: 47.2 us -> none  [shifted(): lax.ppermute(value, axis, [(source, source + steps) for source in range(c...]
    dot_general x5 -> x0, matrix products: 11.2 us -> none  [the longest x1 7.72 us: shards(): terms = jnp.dot(normed, out_weight, preferred_element_type=F32)]
    ppermute x5 -> x0, starting transfers between devices: 6.75 us -> none  [shifted(): lax.ppermute(value, axis, [(source, source + steps) for source in range(c...]
    convert_element_type x2 -> x0, other arithmetic: 2.3 us -> none  [the longest x1 2.09 us: shards(): lax.psum_scatter(terms, 'head', scatter_dimension=1, tiled=True)]
    unnamed x14 -> x11, local copies, waits for them, and re-layouts: 5.1 us -> 3.93 us
  transfers between devices with their start and end apart: 6 -> 0, of which waited for: 5 -> 0; matrix products, arithmetic and copies ran while one was open for 0% -> 0% of each run, Pallas kernels for 0% -> 0%
where the time goes in v2:
time: 95.2 us; the launch traced here: 94.8 us
  Pallas kernels  87.9 us (92%)
  local copies, waits for them, and re-layouts  6.86 us (7%)
    pallas_call x1, Pallas kernels, finish(): pl.pallas_call(finish_kernel, out_shape=jax.ShapeDtypeStruct((tok_local,...  62.3 us
    pallas_call x1, Pallas kernels, local_parts(): pl.pallas_call(local_kernel, grid=(heads_local // HEADS_STEP,), in_specs=...  25.7 us
    unnamed x11, local copies, waits for them, and re-layouts  3.93 us

profile of v2, /device:TPU:27, one launch (start us, length us, event | category | flops | bytes accessed | tf_op | source)
XLA Modules:
  0.0 94.8 jit_solution(13392292927779664926)
XLA Ops:
  0.0 1.5 %reshape.12.k_ref = bf16[512,1024]{1,0:T(8,128)(2,1)S(1)} reshape(bf16[256,2,1024]{2,1,0:T(2,128)(2,1)} %param.9) | data formatting | bytes 2097152 | tf_op jit(solution)/shard_map/reshape | solution.py:216
  1.5 1.5 %reshape.13.v_ref = bf16[512,1024]{1,0:T(8,128)(2,1)S(1)} reshape(bf16[256,2,1024]{2,1,0:T(2,128)(2,1)} %param.10) | data formatting | bytes 2097152 | tf_op jit(solution)/shard_map/reshape | solution.py:217
  3.0 0.0 copy-start
  3.0 1.0 %copy-done = bf16[256,1024]{1,0:T(8,128)(2,1)S(1)} copy-done((bf16[256,1024]{1,0:T(8,128)(2,1)S(1)}, bf16[256,1024]{1,0:T(8,128)(2,1)}, u32[]{:S(2)}) %copy-start) | copy-done | bytes 524312
  4.0 0.0 copy-start.1
  4.0 0.7 copy-done.1
  4.7 0.0 copy-start.2
  4.7 0.7 copy-done.2
  5.4 0.0 copy-start.4
  5.4 0.7 copy-done.4
  6.1 0.0 copy-start.3
  6.1 25.7 %local_blocks.1 = (f32[8,128,128]{2,1,0:T(8,128)S(1)}, f32[8,128,128]{2,1,0:T(8,128)S(1)}, f32[8,256,128]{2,1,0:T(8,128)S(1)}, f32[8,256,128]{2,1,0:T(8,128)S(1)}, f32[2,8,128]{2,1,0:T(8,128)S(1)}) custom-call(bf16[256,1024]{1,0:T(8,128)(2,1)S(1)} %copy-done, bf16[512,1024]{1,0:T(8,128)(2,1)S(1)} %reshape.12.k_ref, bf16[512,1024]{1,0:T(8,128)(2,1)S(1)} %reshape.13.v_ref, ...), custom_call_target="tpu_custom_call" | custom-call | flops 12000000000 | bytes 8000000 | tf_op jit(solution)/shard_map/local_blocks/pallas_call | solution.py:197
  31.8 0.0 copy-done.3
  31.8 62.3 %chain_and_project.1 = bf16[256,1024]{1,0:T(8,128)(2,1)S(1)} custom-call(f32[8,128,128]{2,1,0:T(8,128)S(1)} %get-tuple-element.10.map_ref, f32[8,128,128]{2,1,0:T(8,128)S(1)} %get-tuple-element.11.add_ref, f32[8,256,128]{2,1,0:T(8,128)S(1)} %get-tuple-element.12.mapped_ref, f32[8,256,128]{2,1,0:T(8,128)S(1)} %get-tuple-element.13.local_ref, ...), custom_call_target="tpu_custom_call" | custom-call | flops 4000000000 | bytes 14000000 | tf_op jit(solution)/shard_map/chain_and_project/pallas_call | solution.py:384
  94.0 0.8 copy.10
Async XLA Ops:
  3.0 1.0 %copy-start = (bf16[256,1024]{1,0:T(8,128)(2,1)S(1)}, bf16[256,1024]{1,0:T(8,128)(2,1)}, u32[]{:S(2)}) copy-start(bf16[256,1024]{1,0:T(8,128)(2,1)} %q_ref.1) | copy-start | bytes 1572868
  4.0 0.7 copy-start.1
  4.7 0.7 copy-start.2
  5.4 0.7 copy-start.4
  6.1 25.7 %copy-start.3 = (f32[1024]{0:T(1024)S(1)}, f32[1024]{0:T(1024)}, u32[]{:S(2)}) copy-start(f32[1024]{0:T(1024)} %param.14) | copy-start | bytes 12292

commit v3 on v2

--- a/solution.py
+++ b/solution.py
@@ -26,15 +26,40 @@
     return jnp.dot(a, b, preferred_element_type=F32)
 
 
-def mul(a, b):
-    a_hi, a_lo = a if isinstance(a, tuple) else halves(a)
-    b_hi, b_lo = b if isinstance(b, tuple) else halves(b)
-    out = one(a_hi, b_hi)
-    if a_lo is not None:
-        out = out + one(a_lo, b_hi)
-    if b_lo is not None:
-        out = out + one(a_hi, b_lo)
-    return out
+def beside_halves(a):
+    return jnp.concatenate(halves(a), axis=1)
+
+
+def under(b):
+    return jnp.concatenate([b, b], axis=0)
+
+
+def folded(product):
+    half = product.shape[1] // 2
+    return product[:, :half] + product[:, half:]
+
+
+def mul_sided(a_sided, b_sided):
+    return folded(one(a_sided, under(b_sided)))
+
+
+def mul_wide(a, b):
+    a_hi, a_lo = halves(a)
+    b_hi, b_lo = halves(b)
+    return one(jnp.concatenate([a_hi, a_lo, a_hi], axis=1), jnp.concatenate([b_hi, b_hi, b_lo], axis=0))
+
+
+def lower_rows(a, size):
+    return jnp.concatenate(
+        [a[at + size : at + 2 * size] for at in range(0, ROWS, 2 * size)], axis=0
+    )
+
+
+def spread_rows(a, size):
+    zero = jnp.zeros((size, a.shape[1]), a.dtype)
+    return jnp.concatenate(
+        [part for at in range(0, ROWS // 2, size) for part in (zero, a[at : at + size])], axis=0
+    )
 
 
 def exact(a, b):
@@ -58,47 +83,39 @@
     weaving = jnp.where(
         row < GROUP, (col == 2 * row).astype(F32), (col == 2 * (row - GROUP) + 1).astype(F32)
     )
-    units = []
-    for which in range(HEADS_STEP):
-        head = step * HEADS_STEP + which
-        logs = log_ref[pl.ds(head, 1), :]
-        first = beta_ref[0, pl.ds(head, 1), :]
-        second = beta_ref[1, pl.ds(head, 1), :]
-        segs = seg_ref[...].astype(F32)
-        for block in range(blocks):
-            units.append((which, block, logs, first, second, segs))
+    units = [(which, block) for which in range(HEADS_STEP) for block in range(blocks)]
+    segs = seg_ref[...].astype(F32)
+    zero = jnp.zeros((1, GROUP), F32)
+    log_rows, beta_rows, seg_rows = [], [], []
+    for which, block in units:
+        head, toks = step * HEADS_STEP + which, slice(block * GROUP, (block + 1) * GROUP)
+        log_row = log_ref[pl.ds(head, 1), :]
+        first, second = (beta_ref[j, pl.ds(head, 1), :] for j in range(2))
+        log_rows.append(jnp.concatenate([log_row[:, toks], zero], axis=1))
+        beta_rows.append(jnp.concatenate([first[:, toks], second[:, toks]], axis=1))
+        seg_rows.append(jnp.concatenate([segs[:, toks], zero], axis=1))
+    count = len(units)
+    log_rows, beta_rows, seg_rows = (jnp.concatenate(r, axis=0) for r in (log_rows, beta_rows, seg_rows))
+    cum_rows = exact(log_rows, summing)
+    strength_rows = exact(beta_rows, weaving)
+    doc_rows = exact(seg_rows, spreading)
+    tok_rows = exact(log_rows, ((row < GROUP) & (row <= col)).astype(F32))
+    columns = jnp.transpose(
+        jnp.concatenate(
+            [cum_rows, strength_rows, doc_rows, tok_rows, seg_rows]
+            + [jnp.zeros((ROWS - 5 * count, ROWS), F32)],
+            axis=0,
+        )
+    )
 
     prepared = []
-    for which, block, logs, first, second, segs in units:
+    for at, (which, block) in enumerate(units):
         toks = slice(block * GROUP, (block + 1) * GROUP)
-        zero = jnp.zeros((1, GROUP), F32)
-        packed = jnp.concatenate(
-            [
-                jnp.concatenate([logs[:, toks], zero], axis=1),
-                jnp.concatenate([first[:, toks], second[:, toks]], axis=1),
-                jnp.concatenate([segs[:, toks], zero], axis=1),
-                jnp.zeros((5, ROWS), F32),
-            ],
-            axis=0,
-        )
-        cum_row = exact(packed, summing)[0:1]
-        beta_row = exact(packed, weaving)[1:2]
-        seg_row = exact(packed, spreading)[2:3]
-        columns = jnp.transpose(
-            jnp.concatenate([cum_row, beta_row, seg_row, jnp.zeros((ROWS - 3, ROWS), F32)], axis=0)
-        )
-        cum_col, beta_col, seg_col = columns[:, 0:1], columns[:, 1:2], columns[:, 2:3]
-        tok_columns = jnp.transpose(
-            jnp.concatenate(
-                [
-                    exact(packed, ((row < GROUP) & (row <= col)).astype(F32))[0:1],
-                    packed[2:3],
-                    jnp.zeros((ROWS - 2, ROWS), F32),
-                ],
-                axis=0,
-            )
-        )[:GROUP]
-        cum_tok, seg_tok = tok_columns[:, 0:1], tok_columns[:, 1:2]
+        cum_row, beta_row, seg_row = (r[at : at + 1] for r in (cum_rows, strength_rows, doc_rows))
+        cum_col, beta_col, seg_col, cum_tok, seg_tok = (
+            columns[:, k * count + at : k * count + at + 1] for k in range(5)
+        )
+        cum_tok, seg_tok = cum_tok[:GROUP], seg_tok[:GROUP]
         start = segs[:, 0:1] if block == 0 else segs[:, block * GROUP - 1 : block * GROUP]
         last_seg = segs[:, (block + 1) * GROUP - 1 : (block + 1) * GROUP]
         cum_last = cum_row[:, ROWS - 1 : ROWS]
@@ -146,19 +163,29 @@
     size = 2
     while size < ROWS:
         below = (row // (2 * size) == col // (2 * size)) & (row // size > col // size)
-        split = [halves(x) for x in inverses]
-        inner = [mul(jnp.where(below, p["lower"], 0.0), s) for p, s in zip(prepared, split)]
-        inverses = [x - mul(s, i) for x, s, i in zip(inverses, split, inner)]
+        sided = [beside_halves(x) for x in inverses]
+        masked = [beside_halves(jnp.where(below, p["lower"], 0.0)) for p in prepared]
+        if size < 16:
+            inner = [beside_halves(mul_sided(m, s)) for m, s in zip(masked, sided)]
+            inverses = [x - mul_sided(s, i) for x, s, i in zip(inverses, sided, inner)]
+        else:
+            inner = [beside_halves(mul_sided(lower_rows(m, size), s)) for m, s in zip(masked, sided)]
+            inner = [spread_rows(i, size) for i in inner]
+            change = [mul_sided(lower_rows(s, size), i) for s, i in zip(sided, inner)]
+            inverses = [x - spread_rows(c, size) for x, c in zip(inverses, change)]
         size *= 2
 
     solved = []
-    for (which, block, *_), p, x in zip(units, prepared, inverses):
+    for (which, block), p, x in zip(units, prepared, inverses):
         values = v_ref[block * ROWS : (block + 1) * ROWS, which * DV : (which + 1) * DV]
-        key_mix = mul(x * p["key_scale"], p["keys"])
-        pseudo = mul(x * p["value_scale"], values)
+        key_mix = one(beside_halves(x * p["key_scale"]), under(p["keys"]))
+        pseudo = one(beside_halves(x * p["value_scale"]), under(values))
         solved.append(jnp.concatenate([key_mix, pseudo], axis=1))
-    reads = [mul(p["scores"], s) for p, s in zip(prepared, solved)]
-    moves = [mul(p["keys_t"], s * p["tail"]) for p, s in zip(prepared, solved)]
+    reads = [mul_wide(p["scores"], s) for p, s in zip(prepared, solved)]
+    moves = []
+    for p, s in zip(prepared, solved):
+        twice = jnp.concatenate([p["keys_t"], p["keys_t"]], axis=1)
+        moves.append(one(twice, jnp.concatenate(halves(s * p["tail"]), axis=0)))
     running = [None] * HEADS_STEP
     for block in range(blocks):
         for which in range(HEADS_STEP):
@@ -170,18 +197,16 @@
                 mapped, local = reach, reads[at][:, DK:]
                 running[which] = jnp.concatenate([block_map, moves[at][:, DK:]], axis=1)
             else:
-                before = halves(running[which])
-                out = mul(reach, before)
-                mapped, local = out[:, :DK], out[:, DK:] + reads[at][:, DK:]
-                turned = mul(block_map, before)
+                out = mul_wide(jnp.concatenate([reach, block_map], axis=0), running[which])
+                mapped, local = out[:GROUP, :DK], out[:GROUP, DK:] + reads[at][:, DK:]
                 running[which] = jnp.concatenate(
-                    [turned[:, :DK], turned[:, DK:] + moves[at][:, DK:]], axis=1
+                    [out[GROUP:, :DK], out[GROUP:, DK:] + moves[at][:, DK:]], axis=1
                 )
-            mapped_ref[which, toks, :] = mapped
+            mapped_ref[which, toks, :] = beside_halves(mapped)
             local_ref[which, toks, :] = local
     for which in range(HEADS_STEP):
-        map_ref[which] = running[which][:, :DK]
-        add_ref[which] = running[which][:, DK:]
+        map_ref[which] = beside_halves(jnp.transpose(running[which][:, :DK]))
+        add_ref[which] = jnp.transpose(running[which][:, DK:])
     segs = seg_ref[...].astype(F32)
     edge_ref[0] = jnp.broadcast_to(segs[:, 0:1], (8, 128))
     edge_ref[1] = jnp.broadcast_to(segs[:, segs.shape[1] - 1 :], (8, 128))
@@ -192,8 +217,8 @@
     heads_local = betas.shape[1]
     lanes = HEADS_STEP * DK
     whole = lambda *shape: pl.BlockSpec(shape, lambda h: (0,) * len(shape))
-    per_head = lambda rows: pl.BlockSpec((HEADS_STEP, rows, DK), lambda h: (h, 0, 0))
-    shape = lambda rows: jax.ShapeDtypeStruct((heads_local, rows, DK), F32)
+    per_head = lambda rows, width: pl.BlockSpec((HEADS_STEP, rows, width), lambda h: (h, 0, 0))
+    shape = lambda rows, width, dtype: jax.ShapeDtypeStruct((heads_local, rows, width), dtype)
     return pl.pallas_call(
         local_kernel,
         grid=(heads_local // HEADS_STEP,),
@@ -205,10 +230,21 @@
             whole(heads_local, tok_local),
             whole(1, tok_local),
         ],
-        out_specs=[per_head(DK), per_head(DK), per_head(tok_local), per_head(tok_local), whole(2, 8, 128)],
-        out_shape=[shape(DK), shape(DK), shape(tok_local), shape(tok_local)]
-        + [jax.ShapeDtypeStruct((2, 8, 128), F32)],
-        compiler_params=pltpu.CompilerParams(vmem_limit_bytes=48 * 1024 * 1024),
+        out_specs=[
+            per_head(DK, 2 * DK),
+            per_head(DV, DK),
+            per_head(tok_local, 2 * DK),
+            per_head(tok_local, DV),
+            whole(2, 8, 128),
+        ],
+        out_shape=[
+            shape(DK, 2 * DK, BF16),
+            shape(DV, DK, F32),
+            shape(tok_local, 2 * DK, BF16),
+            shape(tok_local, DV, F32),
+            jax.ShapeDtypeStruct((2, 8, 128), F32),
+        ],
+        compiler_params=pltpu.CompilerParams(vmem_limit_bytes=60 * 1024 * 1024),
         cost_estimate=pl.CostEstimate(flops=12 * 10**9, bytes_accessed=8 * 10**6, transcendentals=10**6),
         name="local_blocks",
     )(
@@ -223,6 +259,7 @@
 
 MESH = pl.DeviceIdType.MESH
 CHUNK = 256
+PIECES = 2
 
 
 def finish_kernel(
@@ -235,6 +272,7 @@
     heads = map_ref.shape[0]
     width = out_ref.shape[1]
     chunks = width // CHUNK
+    rows = DV // PIECES
     beside = mine + 1 - 2 * lax.rem(mine, 2)
     across = lax.rem(mine + 2, 4)
     diagonal = 3 - mine
@@ -262,17 +300,17 @@
         device_id=(after, mine), device_id_type=MESH,
     )
 
-    def state_copy(head):
+    def state_copy(head, piece):
         return pltpu.make_async_remote_copy(
-            src_ref=leaving.at[head], dst_ref=states.at[head],
-            send_sem=chain_send.at[head], recv_sem=chain_recv.at[head],
+            src_ref=leaving.at[head, piece], dst_ref=states.at[head, piece],
+            send_sem=chain_send.at[head, piece], recv_sem=chain_recv.at[head, piece],
             device_id=(after, mine), device_id_type=MESH,
         )
 
     def attend(head, state):
         attended = local_ref[head]
         if state is not None:
-            attended = attended + mul(mapped_ref[head], state)
+            attended = attended + mul_sided(mapped_ref[head], beside_halves(jnp.transpose(state)))
         inverse_rms = 1.0 / jnp.sqrt(jnp.mean(attended * attended, axis=-1, keepdims=True) + 1e-06)
         lanes = pl.ds(pl.multiple_of(head * DV, DV), DV)
         normed[:, lanes] = (attended * inverse_rms * gain_ref[:, lanes]).astype(BF16)
@@ -282,8 +320,9 @@
         seg_copy.start()
 
         def first(head, carry):
-            leaving[head] = add_ref[head]
-            state_copy(head).start()
+            for piece in range(PIECES):
+                leaving[head, piece] = add_ref[head, piece * rows : (piece + 1) * rows, :]
+                state_copy(head, piece).start()
             return carry
 
         lax.fori_loop(0, heads, first, 0)
@@ -304,15 +343,20 @@
         linked = seg_in[0:1, :] == edge_ref[0, 0:1, :]
 
         def link(head, carry):
-            state_copy(head).wait_recv()
-            state = halves(jnp.where(linked, states[head], 0.0))
-
-            @pl.when(has_after)
-            def _():
-                leaving[head] = mul(map_ref[head], state) + add_ref[head]
-                state_copy(head).start()
-
-            attend(head, state)
+            carried = map_ref[head]
+            whole = []
+            for piece in range(PIECES):
+                added = add_ref[head, piece * rows : (piece + 1) * rows, :]
+                state_copy(head, piece).wait_recv()
+                state = jnp.where(linked, states[head, piece], 0.0)
+                whole.append(state)
+
+                @pl.when(has_after)
+                def _():
+                    leaving[head, piece] = mul_sided(beside_halves(state), carried) + added
+                    state_copy(head, piece).start()
+
+            attend(head, jnp.concatenate(whole, axis=0))
             return carry
 
         lax.fori_loop(0, heads, link, 0)
@@ -369,7 +413,8 @@
         seg_copy.wait_send()
 
         def sent(head, carry):
-            state_copy(head).wait_send()
+            for piece in range(PIECES):
+                state_copy(head, piece).wait_send()
             return carry
 
         lax.fori_loop(0, heads, sent, 0)
@@ -389,8 +434,8 @@
         scratch_shapes=[
             pltpu.VMEM(out_weight.shape, BF16),
             pltpu.VMEM((tok_local, heads * DV), BF16),
-            pltpu.VMEM((heads, DK, DV), F32),
-            pltpu.VMEM((heads, DK, DV), F32),
+            pltpu.VMEM((heads, PIECES, DV // PIECES, DK), F32),
+            pltpu.VMEM((heads, PIECES, DV // PIECES, DK), F32),
             pltpu.VMEM((8, 128), F32),
             pltpu.VMEM((2, chunks, tok_local, CHUNK), F32),
             pltpu.VMEM((2, chunks, tok_local, CHUNK), F32),
@@ -399,15 +444,15 @@
             dma,
             dma,
             dma,
-            dma((heads,)),
-            dma((heads,)),
+            dma((heads, PIECES)),
+            dma((heads, PIECES)),
             dma((2, chunks)),
             dma((2, chunks)),
             dma((chunks,)),
             dma((chunks,)),
         ],
         compiler_params=pltpu.CompilerParams(
-            vmem_limit_bytes=48 * 1024 * 1024, collective_id=0, has_side_effects=True
+            vmem_limit_bytes=60 * 1024 * 1024, collective_id=0, has_side_effects=True
         ),
         cost_estimate=pl.CostEstimate(flops=4 * 10**9, bytes_accessed=14 * 10**6, transcendentals=10**4),
         name="chain_and_project",

time: 95.2 us -> 93.9 us (0.986)
    unnamed x11 -> x1, local copies, waits for them, and re-layouts: 3.93 us -> 1.87 us
    pallas_call x1, Pallas kernels: 25.7 us -> 24.3 us  [local_parts(): pl.pallas_call(local_kernel, grid=(heads_local // HEADS_STEP,), in_specs=...]
where the time goes in v3:
time: 93.9 us; the launch traced here: 93.7 us
  Pallas kernels  87.3 us (93%)
  local copies, waits for them, and re-layouts  6.4 us (7%)
    pallas_call x1, Pallas kernels, finish(): pl.pallas_call(finish_kernel, out_shape=jax.ShapeDtypeStruct((tok_local,...  62.9 us
    pallas_call x1, Pallas kernels, local_parts(): pl.pallas_call(local_kernel, grid=(heads_local // HEADS_STEP,), in_specs=...  24.3 us
    reshape x1, local copies, waits for them, and re-layouts, local_parts(): values.reshape(2 * tok_local, -1)  2.26 us
    reshape x1, local copies, waits for them, and re-layouts, local_parts(): keys.reshape(2 * tok_local, -1)  2.26 us

profile of v3, /device:TPU:27, one launch (start us, length us, event | category | flops | bytes accessed | tf_op | source)
XLA Modules:
  0.0 93.7 jit_solution(2775551503501599853)
XLA Ops:
  0.0 2.3 %reshape.12.k_ref = bf16[512,1024]{1,0:T(8,128)(2,1)} reshape(bf16[256,2,1024]{2,1,0:T(2,128)(2,1)} %param.9) | data formatting | bytes 2097152 | tf_op jit(solution)/shard_map/reshape | solution.py:252
  2.3 2.3 %reshape.13.v_ref = bf16[512,1024]{1,0:T(8,128)(2,1)} reshape(bf16[256,2,1024]{2,1,0:T(2,128)(2,1)} %param.10) | data formatting | bytes 2097152 | tf_op jit(solution)/shard_map/reshape | solution.py:253
  4.5 24.3 %local_blocks.1 = (bf16[8,128,256]{2,1,0:T(8,128)(2,1)}, f32[8,128,128]{2,1,0:T(8,128)}, bf16[8,256,256]{2,1,0:T(8,128)(2,1)}, f32[8,256,128]{2,1,0:T(8,128)}, f32[2,8,128]{2,1,0:T(8,128)}) custom-call(bf16[256,1024]{1,0:T(8,128)(2,1)} %q_ref.1, bf16[512,1024]{1,0:T(8,128)(2,1)} %reshape.12.k_ref, bf16[512,1024]{1,0:T(8,128)(2,1)} %reshape.13.v_ref, ...), custom_call_target="tpu_custom_call" | custom-call | flops 12000000000 | bytes 8000000 | tf_op jit(solution)/shard_map/local_blocks/pallas_call | solution.py:222
  28.9 62.9 %chain_and_project.1 = bf16[256,1024]{1,0:T(8,128)(2,1)} custom-call(bf16[8,128,256]{2,1,0:T(8,128)(2,1)} %get-tuple-element.10.map_ref, f32[8,128,128]{2,1,0:T(8,128)} %get-tuple-element.11.add_ref, bf16[8,256,256]{2,1,0:T(8,128)(2,1)} %get-tuple-element.12.mapped_ref, f32[8,256,128]{2,1,0:T(8,128)} %get-tuple-element.13.local_ref, ...), custom_call_target="tpu_custom_call" | custom-call | flops 4000000000 | bytes 14000000 | tf_op jit(solution)/shard_map/chain_and_project/pallas_call | solution.py:429
  91.8 1.9 %copy.10 = bf16[256,1024]{1,0:T(8,128)(2,1)} copy(bf16[256,1024]{1,0:T(8,128)(2,1)} %chain_and_project.1) | data formatting | bytes 1048576

commit v4 on v3

--- a/solution.py
+++ b/solution.py
@@ -11,6 +11,7 @@
 GROUP = 64
 ROWS = 2 * GROUP
 HEADS_STEP = 2
+REFINES = 1
 F32 = jnp.float32
 BF16 = jnp.bfloat16
 
@@ -46,7 +47,8 @@
 def mul_wide(a, b):
     a_hi, a_lo = halves(a)
     b_hi, b_lo = halves(b)
-    return one(jnp.concatenate([a_hi, a_lo, a_hi], axis=1), jnp.concatenate([b_hi, b_hi, b_lo], axis=0))
+    both = one(jnp.concatenate([a_hi, a_lo], axis=0), b_hi)
+    return both[: a.shape[0]] + both[a.shape[0] :] + one(a_hi, b_lo)
 
 
 def lower_rows(a, size):
@@ -161,19 +163,25 @@
 
     inverses = [eye - jnp.where(row // 2 == col // 2, p["lower"], 0.0) for p in prepared]
     size = 2
+    lowers = [p["lower"].astype(BF16) for p in prepared]
+    nothing = jnp.zeros((ROWS, ROWS), BF16)
     while size < ROWS:
         below = (row // (2 * size) == col // (2 * size)) & (row // size > col // size)
-        sided = [beside_halves(x) for x in inverses]
-        masked = [beside_halves(jnp.where(below, p["lower"], 0.0)) for p in prepared]
+        rounded = [x.astype(BF16) for x in inverses]
+        masked = [jnp.where(below, low, nothing) for low in lowers]
         if size < 16:
-            inner = [beside_halves(mul_sided(m, s)) for m, s in zip(masked, sided)]
-            inverses = [x - mul_sided(s, i) for x, s, i in zip(inverses, sided, inner)]
+            inner = [one(m, x).astype(BF16) for m, x in zip(masked, rounded)]
+            inverses = [x - one(r, i) for x, r, i in zip(inverses, rounded, inner)]
         else:
-            inner = [beside_halves(mul_sided(lower_rows(m, size), s)) for m, s in zip(masked, sided)]
+            inner = [one(lower_rows(m, size), x).astype(BF16) for m, x in zip(masked, rounded)]
             inner = [spread_rows(i, size) for i in inner]
-            change = [mul_sided(lower_rows(s, size), i) for s, i in zip(sided, inner)]
+            change = [one(lower_rows(r, size), i) for r, i in zip(rounded, inner)]
             inverses = [x - spread_rows(c, size) for x, c in zip(inverses, change)]
         size *= 2
+    for _ in range(REFINES):
+        sided = [beside_halves(x) for x in inverses]
+        off = [eye - x - mul_sided(beside_halves(p["lower"]), s) for x, p, s in zip(inverses, prepared, sided)]
+        inverses = [x + one(s[:, :ROWS], o.astype(BF16)) for x, s, o in zip(inverses, sided, off)]
 
     solved = []
     for (which, block), p, x in zip(units, prepared, inverses):
@@ -181,7 +189,12 @@
         key_mix = one(beside_halves(x * p["key_scale"]), under(p["keys"]))
         pseudo = one(beside_halves(x * p["value_scale"]), under(values))
         solved.append(jnp.concatenate([key_mix, pseudo], axis=1))
-    reads = [mul_wide(p["scores"], s) for p, s in zip(prepared, solved)]
+    reads = []
+    for p, s in zip(prepared, solved):
+        s_hi, s_lo = halves(s)
+        score_hi, score_lo = halves(p["scores"])
+        both = one(jnp.concatenate([score_hi, score_lo], axis=0), s_hi)
+        reads.append(both[:GROUP] + both[GROUP:] + one(score_hi, s_lo))
     moves = []
     for p, s in zip(prepared, solved):
         twice = jnp.concatenate([p["keys_t"], p["keys_t"]], axis=1)
@@ -452,7 +465,7 @@
             dma((chunks,)),
         ],
         compiler_params=pltpu.CompilerParams(
-            vmem_limit_bytes=60 * 1024 * 1024, collective_id=0, has_side_effects=True
+            vmem_limit_bytes=48 * 1024 * 1024, collective_id=0, has_side_effects=True
         ),
         cost_estimate=pl.CostEstimate(flops=4 * 10**9, bytes_accessed=14 * 10**6, transcendentals=10**4),
         name="chain_and_project",

time: 93.9 us -> 94.6 us (level)
  local copies, waits for them, and re-layouts: 6.4 us -> 10.5 us
  Pallas kernels: 87.3 us -> 83.6 us
    unnamed x1 -> x13, local copies, waits for them, and re-layouts: 1.87 us -> 6.02 us
    pallas_call x1, Pallas kernels: 62.9 us -> 60.2 us  [finish(): pl.pallas_call(finish_kernel, out_shape=jax.ShapeDtypeStruct((tok_local,...]
where the time goes in v4:
time: 94.6 us; the launch traced here: 94.2 us
  Pallas kernels  83.6 us (88%)
  local copies, waits for them, and re-layouts  10.5 us (11%)
    pallas_call x1, Pallas kernels, finish(): pl.pallas_call(finish_kernel, out_shape=jax.ShapeDtypeStruct((tok_local,...  60.2 us
    pallas_call x1, Pallas kernels, local_parts(): pl.pallas_call(local_kernel, grid=(heads_local // HEADS_STEP,), in_specs=...  23.4 us
    unnamed x13, local copies, waits for them, and re-layouts  6.02 us
    reshape x1, local copies, waits for them, and re-layouts, local_parts(): values.reshape(2 * tok_local, -1)  2.28 us
    reshape x1, local copies, waits for them, and re-layouts, local_parts(): keys.reshape(2 * tok_local, -1)  2.25 us

profile of v4, /device:TPU:27, one launch (start us, length us, event | category | flops | bytes accessed | tf_op | source)
XLA Modules:
  0.0 94.2 jit_solution(16622123048486751443)
XLA Ops:
  0.0 2.2 %reshape.12.k_ref = bf16[512,1024]{1,0:T(8,128)(2,1)} reshape(bf16[256,2,1024]{2,1,0:T(2,128)(2,1)} %param.9) | data formatting | bytes 2097152 | tf_op jit(solution)/shard_map/reshape | solution.py:265
  2.3 2.3 %reshape.13.v_ref = bf16[512,1024]{1,0:T(8,128)(2,1)} reshape(bf16[256,2,1024]{2,1,0:T(2,128)(2,1)} %param.10) | data formatting | bytes 2097152 | tf_op jit(solution)/shard_map/reshape | solution.py:266
  4.5 0.0 copy-start
  4.5 23.4 %local_blocks.1 = (bf16[8,128,256]{2,1,0:T(8,128)(2,1)}, f32[8,128,128]{2,1,0:T(8,128)}, bf16[8,256,256]{2,1,0:T(8,128)(2,1)}, f32[8,256,128]{2,1,0:T(8,128)}, f32[2,8,128]{2,1,0:T(8,128)}) custom-call(bf16[256,1024]{1,0:T(8,128)(2,1)} %q_ref.1, bf16[512,1024]{1,0:T(8,128)(2,1)} %reshape.12.k_ref, bf16[512,1024]{1,0:T(8,128)(2,1)} %reshape.13.v_ref, ...), custom_call_target="tpu_custom_call" | custom-call | flops 12000000000 | bytes 8000000 | tf_op jit(solution)/shard_map/local_blocks/pallas_call | solution.py:235
  27.9 0.0 copy-done
  27.9 0.0 copy-start.1
  27.9 1.2 %copy-done.1 = bf16[8,256,256]{2,1,0:T(8,128)(2,1)S(1)} copy-done((bf16[8,256,256]{2,1,0:T(8,128)(2,1)S(1)}, bf16[8,256,256]{2,1,0:T(8,128)(2,1)}, u32[]{:S(2)}) %copy-start.1) | copy-done | bytes 1048600
  29.1 0.0 copy-start.2
  29.2 1.2 %copy-done.2 = f32[8,256,128]{2,1,0:T(8,128)S(1)} copy-done((f32[8,256,128]{2,1,0:T(8,128)S(1)}, f32[8,256,128]{2,1,0:T(8,128)}, u32[]{:S(2)}) %copy-start.2) | copy-done | bytes 1048600
  30.4 0.0 copy-start.3
  30.4 1.0 %copy-done.3 = bf16[8,128,256]{2,1,0:T(8,128)(2,1)S(1)} copy-done((bf16[8,128,256]{2,1,0:T(8,128)(2,1)S(1)}, bf16[8,128,256]{2,1,0:T(8,128)(2,1)}, u32[]{:S(2)}) %copy-start.3) | copy-done | bytes 524312
  31.4 0.0 copy-start.4
  31.4 1.0 %copy-done.4 = f32[8,128,128]{2,1,0:T(8,128)S(1)} copy-done((f32[8,128,128]{2,1,0:T(8,128)S(1)}, f32[8,128,128]{2,1,0:T(8,128)}, u32[]{:S(2)}) %copy-start.4) | copy-done | bytes 524312
  32.5 0.0 copy-start.5
  32.5 0.7 copy-done.5
  33.2 60.2 %chain_and_project.1 = bf16[256,1024]{1,0:T(8,128)(2,1)S(1)} custom-call(bf16[8,128,256]{2,1,0:T(8,128)(2,1)S(1)} %copy-done.3, f32[8,128,128]{2,1,0:T(8,128)S(1)} %copy-done.4, bf16[8,256,256]{2,1,0:T(8,128)(2,1)S(1)} %copy-done.1, f32[8,256,128]{2,1,0:T(8,128)S(1)} %copy-done.2, f32[2,8,128]{2,1,0:T(8,128)S(1)} %copy-done.5, f32[1,1024]{1,0:T(1,128)S(1)} %bitcast.2, ...), custom_call_target="tpu_custom_call" | custom-call | flops 4000000000 | bytes 14000000 | tf_op jit(solution)/shard_map/chain_and_project/pallas_call | solution.py:442
  93.4 0.8 copy.10
Async XLA Ops:
  4.5 23.4 %copy-start = (f32[1024]{0:T(1024)S(1)}, f32[1024]{0:T(1024)}, u32[]{:S(2)}) copy-start(f32[1024]{0:T(1024)} %param.14) | copy-start | bytes 12292
  27.9 1.2 %copy-start.1 = (bf16[8,256,256]{2,1,0:T(8,128)(2,1)S(1)}, bf16[8,256,256]{2,1,0:T(8,128)(2,1)}, u32[]{:S(2)}) copy-start(bf16[8,256,256]{2,1,0:T(8,128)(2,1)} %get-tuple-element.12.mapped_ref) | copy-start | bytes 3145732
  29.1 1.2 %copy-start.2 = (f32[8,256,128]{2,1,0:T(8,128)S(1)}, f32[8,256,128]{2,1,0:T(8,128)}, u32[]{:S(2)}) copy-start(f32[8,256,128]{2,1,0:T(8,128)} %get-tuple-element.13.local_ref) | copy-start | bytes 3145732
  30.4 1.0 %copy-start.3 = (bf16[8,128,256]{2,1,0:T(8,128)(2,1)S(1)}, bf16[8,128,256]{2,1,0:T(8,128)(2,1)}, u32[]{:S(2)}) copy-start(bf16[8,128,256]{2,1,0:T(8,128)(2,1)} %get-tuple-element.10.map_ref) | copy-start | bytes 1572868
  31.4 1.0 %copy-start.4 = (f32[8,128,128]{2,1,0:T(8,128)S(1)}, f32[8,128,128]{2,1,0:T(8,128)}, u32[]{:S(2)}) copy-start(f32[8,128,128]{2,1,0:T(8,128)} %get-tuple-element.11.add_ref) | copy-start | bytes 1572868
  32.5 0.7 copy-start.5

commit v5 on v4

--- a/solution.py
+++ b/solution.py
@@ -10,8 +10,8 @@
 DV = 128
 GROUP = 64
 ROWS = 2 * GROUP
-HEADS_STEP = 2
-REFINES = 1
+HEADS_STEP = 4
+REFINES = 2
 F32 = jnp.float32
 BF16 = jnp.bfloat16
 
@@ -80,8 +80,10 @@
     row_tok = lax.broadcasted_iota(jnp.int32, (GROUP, ROWS), 0)
     col_tok = lax.broadcasted_iota(jnp.int32, (GROUP, ROWS), 1)
     eye = (row == col).astype(F32)
-    summing = ((row < GROUP) & (row <= col // 2)).astype(F32)
-    spreading = ((row < GROUP) & (row == col // 2)).astype(F32)
+    apart = row ^ col
+    half_col = col >> 1
+    summing = ((row < GROUP) & (row <= half_col)).astype(F32)
+    spreading = ((row < GROUP) & (row == half_col)).astype(F32)
     weaving = jnp.where(
         row < GROUP, (col == 2 * row).astype(F32), (col == 2 * (row - GROUP) + 1).astype(F32)
     )
@@ -161,12 +163,12 @@
             )
         )
 
-    inverses = [eye - jnp.where(row // 2 == col // 2, p["lower"], 0.0) for p in prepared]
+    inverses = [eye - jnp.where(apart < 2, p["lower"], 0.0) for p in prepared]
     size = 2
     lowers = [p["lower"].astype(BF16) for p in prepared]
     nothing = jnp.zeros((ROWS, ROWS), BF16)
     while size < ROWS:
-        below = (row // (2 * size) == col // (2 * size)) & (row // size > col // size)
+        below = (row > col) & (apart >= size) & (apart < 2 * size)
         rounded = [x.astype(BF16) for x in inverses]
         masked = [jnp.where(below, low, nothing) for low in lowers]
         if size < 16:
@@ -257,7 +259,7 @@
             shape(tok_local, DV, F32),
             jax.ShapeDtypeStruct((2, 8, 128), F32),
         ],
-        compiler_params=pltpu.CompilerParams(vmem_limit_bytes=60 * 1024 * 1024),
+        compiler_params=pltpu.CompilerParams(vmem_limit_bytes=48 * 1024 * 1024),
         cost_estimate=pl.CostEstimate(flops=12 * 10**9, bytes_accessed=8 * 10**6, transcendentals=10**6),
         name="local_blocks",
     )(

time: 94.6 us -> 85.4 us (0.903)
  Pallas kernels: 83.6 us -> 78.2 us
  local copies, waits for them, and re-layouts: 10.5 us -> 6.86 us
    pallas_call x1, Pallas kernels: 23.4 us -> 17.9 us  [local_parts(): pl.pallas_call(local_kernel, grid=(heads_local // HEADS_STEP,), in_specs=...]
    unnamed x13 -> x11, local copies, waits for them, and re-layouts: 6.02 us -> 3.93 us
where the time goes in v5:
time: 85.4 us; the launch traced here: 85.1 us
  Pallas kernels  78.2 us (92%)
  local copies, waits for them, and re-layouts  6.86 us (8%)
    pallas_call x1, Pallas kernels, finish(): pl.pallas_call(finish_kernel, out_shape=jax.ShapeDtypeStruct((tok_local,...  60.3 us
    pallas_call x1, Pallas kernels, local_parts(): pl.pallas_call(local_kernel, grid=(heads_local // HEADS_STEP,), in_specs=...  17.9 us
    unnamed x11, local copies, waits for them, and re-layouts  3.93 us

profile of v5, /device:TPU:27, one launch (start us, length us, event | category | flops | bytes accessed | tf_op | source)
XLA Modules:
  0.0 85.1 jit_solution(2448116271624073694)
XLA Ops:
  0.0 1.5 %reshape.12.k_ref = bf16[512,1024]{1,0:T(8,128)(2,1)S(1)} reshape(bf16[256,2,1024]{2,1,0:T(2,128)(2,1)} %param.9) | data formatting | bytes 2097152 | tf_op jit(solution)/shard_map/reshape | solution.py:267
  1.5 1.5 %reshape.13.v_ref = bf16[512,1024]{1,0:T(8,128)(2,1)S(1)} reshape(bf16[256,2,1024]{2,1,0:T(2,128)(2,1)} %param.10) | data formatting | bytes 2097152 | tf_op jit(solution)/shard_map/reshape | solution.py:268
  3.0 0.0 copy-start
  3.0 1.0 %copy-done = bf16[256,1024]{1,0:T(8,128)(2,1)S(1)} copy-done((bf16[256,1024]{1,0:T(8,128)(2,1)S(1)}, bf16[256,1024]{1,0:T(8,128)(2,1)}, u32[]{:S(2)}) %copy-start) | copy-done | bytes 524312
  4.0 0.0 copy-start.1
  4.0 0.7 copy-done.1
  4.7 0.0 copy-start.2
  4.7 0.7 copy-done.2
  5.4 0.0 copy-start.4
  5.4 0.7 copy-done.4
  6.1 0.0 copy-start.3
  6.1 17.9 %local_blocks.1 = (bf16[8,128,256]{2,1,0:T(8,128)(2,1)S(1)}, f32[8,128,128]{2,1,0:T(8,128)S(1)}, bf16[8,256,256]{2,1,0:T(8,128)(2,1)S(1)}, f32[8,256,128]{2,1,0:T(8,128)S(1)}, f32[2,8,128]{2,1,0:T(8,128)S(1)}) custom-call(bf16[256,1024]{1,0:T(8,128)(2,1)S(1)} %copy-done, bf16[512,1024]{1,0:T(8,128)(2,1)S(1)} %reshape.12.k_ref, ...), custom_call_target="tpu_custom_call" | custom-call | flops 12000000000 | bytes 8000000 | tf_op jit(solution)/shard_map/local_blocks/pallas_call | solution.py:237
  24.0 0.0 copy-done.3
  24.0 60.3 %chain_and_project.1 = bf16[256,1024]{1,0:T(8,128)(2,1)S(1)} custom-call(bf16[8,128,256]{2,1,0:T(8,128)(2,1)S(1)} %get-tuple-element.10.map_ref, f32[8,128,128]{2,1,0:T(8,128)S(1)} %get-tuple-element.11.add_ref, bf16[8,256,256]{2,1,0:T(8,128)(2,1)S(1)} %get-tuple-element.12.mapped_ref, f32[8,256,128]{2,1,0:T(8,128)S(1)} %get-tuple-element.13.local_ref, ...), custom_call_target="tpu_custom_call" | custom-call | flops 4000000000 | bytes 14000000 | tf_op jit(solution)/shard_map/chain_and_project/pallas_call | solution.py:444
  84.3 0.8 copy.10
Async XLA Ops:
  3.0 1.0 %copy-start = (bf16[256,1024]{1,0:T(8,128)(2,1)S(1)}, bf16[256,1024]{1,0:T(8,128)(2,1)}, u32[]{:S(2)}) copy-start(bf16[256,1024]{1,0:T(8,128)(2,1)} %q_ref.1) | copy-start | bytes 1572868
  4.0 0.7 copy-start.1
  4.7 0.7 copy-start.2
  5.4 0.7 copy-start.4
  6.1 17.9 %copy-start.3 = (f32[1024]{0:T(1024)S(1)}, f32[1024]{0:T(1024)}, u32[]{:S(2)}) copy-start(f32[1024]{0:T(1024)} %param.14) | copy-start | bytes 12292

commit v6 on v5

--- a/solution.py
+++ b/solution.py
@@ -166,11 +166,11 @@
     inverses = [eye - jnp.where(apart < 2, p["lower"], 0.0) for p in prepared]
     size = 2
     lowers = [p["lower"].astype(BF16) for p in prepared]
-    nothing = jnp.zeros((ROWS, ROWS), BF16)
     while size < ROWS:
         below = (row > col) & (apart >= size) & (apart < 2 * size)
         rounded = [x.astype(BF16) for x in inverses]
-        masked = [jnp.where(below, low, nothing) for low in lowers]
+        kept = below.astype(F32).astype(BF16)
+        masked = [low * kept for low in lowers]
         if size < 16:
             inner = [one(m, x).astype(BF16) for m, x in zip(masked, rounded)]
             inverses = [x - one(r, i) for x, r, i in zip(inverses, rounded, inner)]

time: 85.4 us -> 85.5 us (level)
  no operation moved by 1% of the time
where the time goes in v6:
time: 85.5 us; the launch traced here: 85.2 us
  Pallas kernels  78.3 us (92%)
  local copies, waits for them, and re-layouts  6.86 us (8%)
    pallas_call x1, Pallas kernels, finish(): pl.pallas_call(finish_kernel, out_shape=jax.ShapeDtypeStruct((tok_local,...  60.3 us
    pallas_call x1, Pallas kernels, local_parts(): pl.pallas_call(local_kernel, grid=(heads_local // HEADS_STEP,), in_specs=...  18 us
    unnamed x11, local copies, waits for them, and re-layouts  3.93 us

profile of v6, /device:TPU:27, one launch (start us, length us, event | category | flops | bytes accessed | tf_op | source)
XLA Modules:
  0.0 85.2 jit_solution(3963920808496817771)
XLA Ops:
  0.0 1.5 %reshape.12.k_ref = bf16[512,1024]{1,0:T(8,128)(2,1)S(1)} reshape(bf16[256,2,1024]{2,1,0:T(2,128)(2,1)} %param.9) | data formatting | bytes 2097152 | tf_op jit(solution)/shard_map/reshape | solution.py:267
  1.5 1.5 %reshape.13.v_ref = bf16[512,1024]{1,0:T(8,128)(2,1)S(1)} reshape(bf16[256,2,1024]{2,1,0:T(2,128)(2,1)} %param.10) | data formatting | bytes 2097152 | tf_op jit(solution)/shard_map/reshape | solution.py:268
  3.0 0.0 copy-start
  3.0 1.0 %copy-done = bf16[256,1024]{1,0:T(8,128)(2,1)S(1)} copy-done((bf16[256,1024]{1,0:T(8,128)(2,1)S(1)}, bf16[256,1024]{1,0:T(8,128)(2,1)}, u32[]{:S(2)}) %copy-start) | copy-done | bytes 524312
  4.0 0.0 copy-start.1
  4.0 0.7 copy-done.1
  4.7 0.0 copy-start.2
  4.7 0.7 copy-done.2
  5.4 0.0 copy-start.4
  5.4 0.7 copy-done.4
  6.1 0.0 copy-start.3
  6.1 18.0 %local_blocks.1 = (bf16[8,128,256]{2,1,0:T(8,128)(2,1)S(1)}, f32[8,128,128]{2,1,0:T(8,128)S(1)}, bf16[8,256,256]{2,1,0:T(8,128)(2,1)S(1)}, f32[8,256,128]{2,1,0:T(8,128)S(1)}, f32[2,8,128]{2,1,0:T(8,128)S(1)}) custom-call(bf16[256,1024]{1,0:T(8,128)(2,1)S(1)} %copy-done, bf16[512,1024]{1,0:T(8,128)(2,1)S(1)} %reshape.12.k_ref, ...), custom_call_target="tpu_custom_call" | custom-call | flops 12000000000 | bytes 8000000 | tf_op jit(solution)/shard_map/local_blocks/pallas_call | solution.py:237
  24.1 0.0 copy-done.3
  24.1 60.3 %chain_and_project.1 = bf16[256,1024]{1,0:T(8,128)(2,1)S(1)} custom-call(bf16[8,128,256]{2,1,0:T(8,128)(2,1)S(1)} %get-tuple-element.10.map_ref, f32[8,128,128]{2,1,0:T(8,128)S(1)} %get-tuple-element.11.add_ref, bf16[8,256,256]{2,1,0:T(8,128)(2,1)S(1)} %get-tuple-element.12.mapped_ref, f32[8,256,128]{2,1,0:T(8,128)S(1)} %get-tuple-element.13.local_ref, ...), custom_call_target="tpu_custom_call" | custom-call | flops 4000000000 | bytes 14000000 | tf_op jit(solution)/shard_map/chain_and_project/pallas_call | solution.py:444
  84.4 0.8 copy.10
Async XLA Ops:
  3.0 1.0 %copy-start = (bf16[256,1024]{1,0:T(8,128)(2,1)S(1)}, bf16[256,1024]{1,0:T(8,128)(2,1)}, u32[]{:S(2)}) copy-start(bf16[256,1024]{1,0:T(8,128)(2,1)} %q_ref.1) | copy-start | bytes 1572868
  4.0 0.7 copy-start.1
  4.7 0.7 copy-start.2
  5.4 0.7 copy-start.4
  6.1 18.0 %copy-start.3 = (f32[1024]{0:T(1024)S(1)}, f32[1024]{0:T(1024)}, u32[]{:S(2)}) copy-start(f32[1024]{0:T(1024)} %param.14) | copy-start | bytes 12292
